TPU v7x, 32 devices: a whole 2x2x4 slice. The times are simulated.
32 devices in a mesh: vocab: 16 (over z, y, x), rows: 2 (over core).
Axes of the slice: x: 2, y: 2, z: 4, core: 2. Of those that a mesh axis runs over, the one named last changes fastest.
Arguments:
- hidden: bfloat16 [512, 4096], P('rows', 'vocab'), may hold values from -64 to 64
- head_weight: bfloat16 [4096, 16384], P(None, 'vocab'), may hold values from -0.09375 to 0.09375
- mentor_outputs: bfloat16 [512, 16384], P('rows', 'vocab'), may hold values from -480 to 480
Outputs:
- hidden_grad: bfloat16 [512, 4096], P('rows', 'vocab')
- weight_grad: bfloat16 [4096, 16384], P('rows', 'vocab')
- per_position_mismatch: float32 [512], P('rows')
All inputs are finite; a program needn't handle non-finite values.
Results may differ from a plain program's by a relative error of at most 0.0043.
Values may be sent and summed in bfloat16 or wider, within the bound.
A program may use at most 128 MiB of HBM per device.

v0:
```python
import jax
import jax.numpy as jnp
from jax import lax
from jax.sharding import PartitionSpec as P

sharpness_divisor = 2.0
objective_factor = 32.0


def shards(hidden, head_weight, mentor_outputs):
    full_hidden = lax.all_gather(hidden, "vocab", axis=1, tiled=True)
    unnormalized_outputs = jnp.dot(full_hidden, head_weight, preferred_element_type=jnp.float32)
    learner_raw_outputs = unnormalized_outputs / sharpness_divisor
    mentor_raw_outputs = mentor_outputs.astype(jnp.float32) / sharpness_divisor
    top_s, top_t = lax.pmax(
        (jnp.max(learner_raw_outputs, axis=1), jnp.max(mentor_raw_outputs, axis=1)), "vocab"
    )
    exp_s = jnp.exp(learner_raw_outputs - top_s[:, None])
    exp_t = jnp.exp(mentor_raw_outputs - top_t[:, None])
    total_s, total_t, weighted = lax.psum(
        (
            jnp.sum(exp_s, axis=1),
            jnp.sum(exp_t, axis=1),
            jnp.sum(exp_t * (mentor_raw_outputs - learner_raw_outputs), axis=1),
        ),
        "vocab",
    )
    learner_partition_value = top_s + jnp.log(total_s)
    mentor_partition_value = top_t + jnp.log(total_t)
    mismatch_summand = weighted / total_t
    per_position_mismatch = (
        sharpness_divisor
        * sharpness_divisor
        * (mismatch_summand + learner_partition_value - mentor_partition_value)
    )
    learner_likelihood = jnp.exp(learner_raw_outputs - learner_partition_value[:, None])
    mentor_likelihood = jnp.exp(mentor_raw_outputs - mentor_partition_value[:, None])
    raw_score_derivative = (
        objective_factor * sharpness_divisor * (learner_likelihood - mentor_likelihood)
    ).astype(jnp.bfloat16)
    hidden_part = lax.psum_scatter(
        lax.dot_general(
            head_weight,
            raw_score_derivative,
            (((1,), (1,)), ((), ())),
            preferred_element_type=jnp.float32,
        ),
        "vocab",
        scatter_dimension=0,
        tiled=True,
    )
    hidden_grad = hidden_part.T.astype(jnp.bfloat16)
    weight_grad = lax.psum_scatter(
        lax.dot_general(
            full_hidden,
            raw_score_derivative,
            (((0,), (0,)), ((), ())),
            preferred_element_type=jnp.float32,
        ),
        "rows",
        scatter_dimension=0,
        tiled=True,
    ).astype(jnp.bfloat16)
    return (hidden_grad, weight_grad, per_position_mismatch)


def solution(mesh):
    placed = (P("rows", "vocab"), P(None, "vocab"), P("rows", "vocab"))
    return jax.shard_map(
        shards,
        mesh=mesh,
        in_specs=placed,
        out_specs=(P("rows", "vocab"), P("rows", "vocab"), P("rows")),
        check_vma=False,
    )
```

profile of v0, /device:TPU:0, one launch (start us, length us, event | category | flops | bytes accessed | tf_op | source)
XLA Modules:
  0.0 309.7 jit_solution(8812890516849982390)
XLA Ops:
  7.2 0.0 all-gather.2.cloned.1.call-start
  7.2 0.7 all-gather.2.cloned.1.call-update
  7.9 0.0 reduce-scatter.3.cloned.1.call-start
  7.9 1.2 fusion.1
  9.2 0.0 copy-start
  9.2 69.4 %all-gather.2.cloned.1.call-done = bf16[256,4096]{1,0:T(8,128)(2,1)} async-done(((bf16[256,256]{1,0:T(8,128)(2,1)}), bf16[256,4096]{1,0:T(8,128)(2,1)}) %all-gather.2.cloned.1.call-update) | async-done | bytes 2097168 | tf_op jit(solution)/shard_map/all_gather | solution.py:11
  78.6 6.4 %fusion.2 = (f32[256]{0:T(256)S(1)}, f32[256,1024]{1,0:T(8,128)S(1)}) fusion(bf16[256,4096]{1,0:T(8,128)(2,1)} %all-gather.2.cloned.1.call-done, bf16[4096,1024]{1,0:T(8,128)(2,1)} %param.4), kind=kOutput, calls=%fused_computation.14 | convolution fusion | flops 2148007680 | bytes 11535360 | tf_op jit(solution)/shard_map/dot_general | solution.py:12
  85.0 38.7 %all-reduce.1 = (f32[256]{0:T(256)S(1)}, f32[256]{0:T(256)S(1)}) all-reduce(f32[256]{0:T(256)S(1)} %fusion.1, f32[256]{0:T(256)S(1)} %get-tuple-element.17), channel_id=1, replica_groups=mesh['vocab'=16,'rows'=2] {'vocab'}, use_global_device_ids=true, to_apply=%region_5.0 | all-reduce | flops 512 | bytes 4096 | tf_op jit(solution)/shard_map/pmax | solution.py:15
  123.7 0.0 copy-done
  123.7 0.7 multiply_reduce_fusion
  124.4 36.6 %all-reduce = (f32[256]{0:T(256)S(1)}, f32[256]{0:T(256)S(1)}, f32[256]{0:T(256)S(1)}) all-reduce(f32[256]{0:T(256)S(1)} %get-tuple-element.8, f32[256]{0:T(256)S(1)} %get-tuple-element.7, f32[256]{0:T(256)S(1)} %get-tuple-element.6), channel_id=1, replica_groups=mesh['vocab'=16,'rows'=2] {'vocab'}, use_global_device_ids=true, to_apply=%region_7.0 | all-reduce | flops 768 | bytes 6144 | tf_op jit(solution)/shard_map/psum | solution.py:20
  161.0 0.6 subtract_multiply_fusion
  161.5 8.0 %convolution_bitcast_fusion.1 = f32[4096,256]{0,1:T(8,128)} fusion(bf16[4096,1024]{1,0:T(8,128)(2,1)} %param.4, bf16[256,1024]{1,0:T(8,128)(2,1)S(1)} %copy-done, f32[256,1024]{1,0:T(8,128)S(1)} %get-tuple-element.18, f32[256]{0:T(256)S(1)} %get-tuple-element.16, f32[256]{0:T(256)S(1)} %get-tuple-element.15), kind=kOutput, calls=%fused_computation.1 | convolution fusion | flops 2149318656 | bytes 14157824 | tf_op jit(solution)/shard_map/dot_general | solution.py:42
  169.5 0.0 reduce-scatter.3.cloned.1.call-update
  169.5 0.0 reduce-scatter.5.cloned.1.call-start
  169.6 9.9 %convolution_bitcast_fusion = f32[4096,1024]{0,1:T(8,128)} fusion(bf16[256,4096]{1,0:T(8,128)(2,1)} %all-gather.2.cloned.1.call-done, bf16[256,1024]{1,0:T(8,128)(2,1)S(1)} %copy-done, f32[256,1024]{1,0:T(8,128)S(1)} %get-tuple-element.18, f32[256]{0:T(256)S(1)} %get-tuple-element.16, f32[256]{0:T(256)S(1)} %get-tuple-element.15), kind=kOutput, calls=%fused_computation | convolution fusion | flops 2149318656 | bytes 20449280 | tf_op jit(solution)/shard_map/dot_general | solution.py:54
  179.5 0.0 reduce-scatter.5.cloned.1.call-update
  179.5 83.0 %reduce-scatter.3.cloned.1.call-done = f32[256,256]{0,1:T(8,128)} async-done(((f32[4096,256]{0,1:T(8,128)}), f32[256,256]{0,1:T(8,128)}) %reduce-scatter.3.cloned.1.call-update) | async-done | bytes 262160 | tf_op jit(solution)/shard_map/reduce_scatter | solution.py:41
  262.6 1.6 convert_bitcast_fusion
  264.2 26.6 %reduce-scatter.5.cloned.1.call-done = f32[2048,1024]{0,1:T(8,128)} async-done(((f32[4096,1024]{0,1:T(8,128)}), f32[2048,1024]{0,1:T(8,128)}) %reduce-scatter.5.cloned.1.call-update) | async-done | bytes 8388624 | tf_op jit(solution)/shard_map/reduce_scatter | solution.py:53
  290.8 6.0 %convert_element_type.19 = bf16[2048,1024]{0,1:T(8,128)(2,1)} convert(f32[2048,1024]{0,1:T(8,128)} %reduce-scatter.5.cloned.1.call-done) | non-fusion elementwise | flops 2097152 | bytes 12582912 | tf_op jit(solution)/shard_map/convert_element_type | solution.py:63
  296.8 6.4 %copy.6 = bf16[2048,1024]{1,0:T(8,128)(2,1)} copy(bf16[2048,1024]{0,1:T(8,128)(2,1)} %convert_element_type.19) | data formatting | bytes 8388608
Async XLA Ops:
  7.2 71.4 %all-gather.2.cloned.1.call-start = ((), (), s32[]{:S(2)}) async-start(), calls=%async_computation.2 | async-start | bytes 2228224 | tf_op jit(solution)/shard_map/all_gather | solution.py:11
  7.9 254.7 %reduce-scatter.3.cloned.1.call-start = ((), (), s32[]{:S(2)}) async-start(), calls=%async_computation.3 | async-start | bytes 4456448 | tf_op jit(solution)/shard_map/reduce_scatter | solution.py:41
  9.2 114.6 %copy-start = (bf16[256,1024]{1,0:T(8,128)(2,1)S(1)}, bf16[256,1024]{1,0:T(8,128)(2,1)}, u32[]{:S(2)}) copy-start(bf16[256,1024]{1,0:T(8,128)(2,1)} %param.5) | copy-start | bytes 1572868
  169.5 121.3 %reduce-scatter.5.cloned.1.call-start = ((), (), s32[]{:S(2)}) async-start(), calls=%async_computation.4 | async-start | bytes 25165824 | tf_op jit(solution)/shard_map/reduce_scatter | solution.py:53
Sparse Core Ops, SparseCore 0:
  10.7 67.8 all-gather.1
  169.7 92.8 reduce-scatter.2
  264.9 25.8 reduce-scatter.4
where the time goes:
time: 310 us
  waiting for transfers between devices  180 us (58%)
  blocking collectives  75.3 us (24%)
  matrix products  24.3 us (8%)
  between operations  13.8 us (4%)
  other arithmetic  10 us (3%)
  local copies, waits for them, and re-layouts  6.39 us (2%)
    reduce_scatter x1, waiting for transfers between devices, shards(): lax.psum_scatter(lax.dot_general(head_weight, raw_score_derivative, (((1,...  83 us
    all_gather x1, waiting for transfers between devices, shards(): full_hidden = lax.all_gather(hidden, 'vocab', axis=1, tiled=True)  69.4 us
    pmax x1, blocking collectives, shards(): lax.pmax((jnp.max(learner_raw_outputs, axis=1), jnp.max(mentor_raw_output...  38.7 us
    psum x1, blocking collectives, shards(): lax.psum((jnp.sum(exp_s, axis=1), jnp.sum(exp_t, axis=1), jnp.sum(exp_t *...  36.6 us
    reduce_scatter x1, waiting for transfers between devices, shards(): lax.psum_scatter(lax.dot_general(full_hidden, raw_score_derivative, (((0,...  26.6 us
    dot_general x1, matrix products, shards(): lax.dot_general(full_hidden, raw_score_derivative, (((0,), (0,)), ((), ()...  9.93 us
    dot_general x1, matrix products, shards(): lax.dot_general(head_weight, raw_score_derivative, (((1,), (1,)), ((), ()...  7.98 us
    dot_general x1, matrix products, shards(): jnp.dot(full_hidden, head_weight, preferred_element_type=jnp.float32)  6.43 us
  transfers between devices with their start and end apart: 3, of which 3 were waited for; matrix products, arithmetic and copies ran while one was open for 4% of the time, Pallas kernels for 0%

commit v1 on v0

v1 whole, which is shorter than its diff:
```python
import functools

import jax
import jax.numpy as jnp
from jax import lax
from jax.experimental import pallas as pl
from jax.experimental.pallas import tpu as pltpu
from jax.sharding import PartitionSpec as P

sharpness_divisor = 2.0
objective_factor = 32.0
f32 = jnp.float32
bf16 = jnp.bfloat16

NT = (((1,), (1,)), ((), ()))
TN = (((0,), (0,)), ((), ()))


def stages(h_hbm, w_hbm, t_hbm, hg_ref, wg_hbm, mm_ref,
           gath, pgath, w, t, es, et, score, pscore, cols, rowsbuf, stat,
           sa, ra, sb, rb, pb, q, sd, rd, wgs,
           loc_sem, ag_recv, z_send, xy_send, f_send, st_send, st_recv,
           a_send, a_recv, b_send, b_recv, d_send, d_recv, p_send, p_recv, out_sem):
    n = gath.shape[0]
    tok, width = h_hbm.shape
    half = tok // 2
    me = lax.axis_index("vocab")
    core = lax.axis_index("rows")
    z, y, x = me // 4, lax.rem(me // 2, 2), lax.rem(me, 2)
    mid = jnp.logical_or(z == 1, z == 2)

    def dev(zz, dy, dx):
        yy = 1 - y if dy else y
        xx = 1 - x if dx else x
        return zz * 4 + yy * 2 + xx

    z_near = z + 1 - 2 * lax.rem(z, 2)
    z_in = 3 - z
    low = z // 2
    planes = [z, z_near, 2 - low, 3 - 3 * low]
    xdev, ydev = dev(z, 0, 1), dev(z, 1, 0)

    def remote(src, dst, ss, rs, target):
        return pltpu.make_async_remote_copy(
            src_ref=src, dst_ref=dst, send_sem=ss, recv_sem=rs,
            device_id={"vocab": target}, device_id_type=pl.DeviceIdType.MESH)

    def partner(src, dst, i):
        return pltpu.make_async_remote_copy(
            src_ref=src, dst_ref=dst, send_sem=p_send.at[i], recv_sem=p_recv.at[i],
            device_id={"rows": 1 - core}, device_id_type=pl.DeviceIdType.MESH)

    cp_h = pltpu.make_async_copy(h_hbm, gath.at[me], loc_sem.at[0])
    cp_w = pltpu.make_async_copy(w_hbm, w, loc_sem.at[1])
    cp_t = pltpu.make_async_copy(t_hbm, t, loc_sem.at[2])
    cp_h.start()
    cp_t.start()
    cp_w.start()

    barrier = pltpu.get_barrier_semaphore()

    def greet(i, c):
        pl.semaphore_signal(barrier, inc=1, device_id={"vocab": lax.rem(me + i, n)},
                            device_id_type=pl.DeviceIdType.MESH)
        return c
    lax.fori_loop(1, n, greet, 0)
    pl.semaphore_signal(barrier, inc=1, device_id={"rows": 1 - core},
                        device_id_type=pl.DeviceIdType.MESH)
    pl.semaphore_wait(barrier, n)
    cp_h.wait()

    def piece(slot, h):
        return gath.at[slot, pl.ds(h * half, half)]

    def gcopy(slot, h, ss, target):
        return remote(piece(slot, h), piece(slot, h), ss, ag_recv.at[slot, h], target)

    def wait_piece(slot, h):
        gcopy(slot, h, f_send.at[0, 0], xdev).wait_recv()

    pending, pending_mid = [], []

    def go(c):
        c.start()
        pending.append(c)

    def go_mid(c):
        pl.when(mid)(c.start)
        pending_mid.append(c)

    def fan_out(i):
        slot = dev(planes[i], 0, 0)
        go(gcopy(slot, 0, xy_send.at[i, 0], ydev))
        go(gcopy(slot, 1, xy_send.at[i, 1], xdev))
        go(gcopy(slot, 1, xy_send.at[i, 2], ydev))
        go(gcopy(slot, 0, xy_send.at[i, 3], xdev))

    def forward(i):
        s0, s1 = dev(planes[i], 1, 0), dev(planes[i], 0, 1)
        wait_piece(s0, 0)
        go(gcopy(s0, 0, f_send.at[i, 0], xdev))
        wait_piece(s1, 1)
        go(gcopy(s1, 1, f_send.at[i, 1], ydev))

    def wrows(slot):
        return pl.ds(pl.multiple_of(slot * width, width), width)

    def multiply(slot, first=False):
        part = jnp.dot(gath[slot], w[wrows(slot), :], preferred_element_type=f32)
        if first:
            es[...] = part
        else:
            es[...] += part

    zn_dev, zi_dev = dev(z_near, 0, 0), dev(z_in, 0, 0)
    for h in range(2):
        go(gcopy(me, h, z_send.at[0, h], zn_dev))
        go_mid(gcopy(me, h, z_send.at[1, h], zi_dev))
    fan_out(0)

    block = 32
    nblk = tok // block
    lane = lax.broadcasted_iota(jnp.int32, (block, 128), 1)
    cp_t.wait()

    def teacher(b, c):
        rows = pl.ds(pl.multiple_of(b * block, block), block)
        tv = t[rows, :].astype(f32) / sharpness_divisor
        m = jnp.max(tv, axis=1, keepdims=True)
        e = jnp.exp(tv - m)
        et[rows, :] = e
        total = jnp.sum(e, axis=1, keepdims=True)
        cols[rows, :] = jnp.where(lane == 2, m, jnp.where(lane == 3, total, 0.0))
        return c
    lax.fori_loop(0, nblk, teacher, 0)

    cp_w.wait()
    multiply(me, True)
    for i in range(1, 4):
        slot = dev(planes[i], 0, 0)
        target = zi_dev if i == 1 else zn_dev
        for h in range(2):
            wait_piece(slot, h)
            go_mid(gcopy(slot, h, z_send.at[1 + i, h], target))
        fan_out(i)
        forward(i - 1)
        multiply(slot)
        if i > 1:
            s0, s1 = dev(planes[i - 2], 1, 0), dev(planes[i - 2], 0, 1)
            wait_piece(s0, 1)
            multiply(s0)
            wait_piece(s1, 0)
            multiply(s1)
    forward(3)
    for i in range(2):
        s = dev(planes[i], 1, 1)
        wait_piece(s, 0)
        wait_piece(s, 1)
        multiply(s)
    for i in range(2, 4):
        s0, s1, s = dev(planes[i], 1, 0), dev(planes[i], 0, 1), dev(planes[i], 1, 1)
        wait_piece(s0, 1)
        multiply(s0)
        wait_piece(s1, 0)
        multiply(s1)
        wait_piece(s, 0)
        wait_piece(s, 1)
        multiply(s)

    mine = n // 2
    ph = partner(gath.at[pl.ds((1 - core) * mine, mine)], pgath, 0)
    ph.start()

    def student(b, c):
        rows = pl.ds(pl.multiple_of(b * block, block), block)
        sv = es[rows, :] / sharpness_divisor
        tv = t[rows, :].astype(f32) / sharpness_divisor
        m = jnp.max(sv, axis=1, keepdims=True)
        e = jnp.exp(sv - m)
        es[rows, :] = e
        total = jnp.sum(e, axis=1, keepdims=True)
        weighted = jnp.sum(et[rows, :] * (tv - sv), axis=1, keepdims=True)
        old = cols[rows, :]
        cols[rows, :] = jnp.where(
            lane == 0, m, jnp.where(lane == 1, total, jnp.where(lane == 4, weighted, old)))
        return c
    lax.fori_loop(0, nblk, student, 0)
    stat[me] = jnp.transpose(cols[...])[:8, :]

    def stat_copy(i):
        return remote(stat.at[me], stat.at[me], st_send.at[i], st_recv.at[me],
                      lax.rem(me + i, n))

    def stat_start(i, c):
        stat_copy(i).start()
        return c
    lax.fori_loop(1, n, stat_start, 0)

    def stat_wait(i, c):
        other = lax.rem(me + i, n)
        remote(stat.at[other], stat.at[other], st_send.at[i], st_recv.at[other],
               other).wait_recv()
        return c
    lax.fori_loop(1, n, stat_wait, 0)

    ms, ss = stat[:, 0:1, :], stat[:, 1:2, :]
    mt, tt, wt = stat[:, 2:3, :], stat[:, 3:4, :], stat[:, 4:5, :]
    top_s, top_t = jnp.max(ms, axis=0), jnp.max(mt, axis=0)
    total_s = jnp.sum(ss * jnp.exp(ms - top_s[None]), axis=0)
    scale_t = jnp.exp(mt - top_t[None])
    total_t = jnp.sum(tt * scale_t, axis=0)
    cross = jnp.sum(wt * scale_t, axis=0) / total_t
    lse_s = top_s + jnp.log(total_s)
    lse_t = top_t + jnp.log(total_t)
    mm_ref[...] = sharpness_divisor * sharpness_divisor * (cross + lse_s - lse_t)
    own = stat[me]
    gain = objective_factor * sharpness_divisor
    rowsbuf[...] = jnp.zeros_like(rowsbuf)
    rowsbuf[0:1, :] = gain * jnp.exp(own[0:1, :] - lse_s)
    rowsbuf[1:2, :] = gain * jnp.exp(own[2:3, :] - lse_t)
    cols[...] = jnp.transpose(rowsbuf[...])

    def derive(b, c):
        rows = pl.ds(pl.multiple_of(b * block, block), block)
        f = cols[rows, :]
        score[rows, :] = (es[rows, :] * f[:, 0:1] - et[rows, :] * f[:, 1:2]).astype(bf16)
        return c
    lax.fori_loop(0, nblk, derive, 0)
    ps = partner(score, pscore, 1)
    ps.start()

    def part(slot):
        return lax.dot_general(score[...], w[wrows(slot), :], NT, preferred_element_type=f32)

    order = [planes[3], planes[2], planes[1], planes[0]]
    for k in range(4):
        p = part(dev(order[k], 1, 1)).astype(bf16)
        sa[k, 0] = p[:half]
        sa[k, 1] = p[half:]
        go(remote(sa.at[k, 0], ra.at[k, 0], a_send.at[k, 0], a_recv.at[k, 0], xdev))
        go(remote(sa.at[k, 1], ra.at[k, 1], a_send.at[k, 1], a_recv.at[k, 1], ydev))

    def bcopy(k, d, h):
        return remote(sb.at[k, d, h], rb.at[k, d, h], b_send.at[k, d, h],
                      b_recv.at[k, d, h], xdev if d else ydev)

    for k in range(4):
        p = part(dev(order[k], 1, 0))
        pb[k, 0] = p[:half]
        sb[k, 0, 1] = p[half:].astype(bf16)
        go(bcopy(k, 0, 1))
        p = part(dev(order[k], 0, 1))
        pb[k, 1] = p[half:]
        sb[k, 1, 0] = p[:half].astype(bf16)
        go(bcopy(k, 1, 0))
    for k in range(4):
        q[k] = part(dev(order[k], 0, 0))

    def weight_part(j, c):
        slot = core * mine + j
        for v in range(2):
            vs = pl.ds(v * (w.shape[1] // 2), w.shape[1] // 2)
            g = lax.dot_general(gath[slot], score[:, vs], TN, preferred_element_type=f32)
            g += lax.dot_general(pgath[j], pscore[:, vs], TN, preferred_element_type=f32)
            wgs[j, :, vs] = g.astype(bf16)
        pltpu.make_async_copy(wgs.at[j], wg_hbm.at[pl.ds(pl.multiple_of(j * width, width), width)],
                              out_sem.at[j]).start()
        return c

    def join(k):
        a = remote(sa.at[k, 0], ra.at[k, 0], a_send.at[k, 0], a_recv.at[k, 0], xdev)
        a.wait_recv()
        sb[k, 0, 0] = (pb[k, 0] + ra[k, 0].astype(f32)).astype(bf16)
        go(bcopy(k, 0, 0))
        a = remote(sa.at[k, 1], ra.at[k, 1], a_send.at[k, 1], a_recv.at[k, 1], ydev)
        a.wait_recv()
        sb[k, 1, 1] = (pb[k, 1] + ra[k, 1].astype(f32)).astype(bf16)
        go(bcopy(k, 1, 1))

    join(0)
    join(1)
    ph.wait()
    ps.wait()
    lax.fori_loop(0, mine // 2, weight_part, 0)
    join(2)
    join(3)
    lax.fori_loop(mine // 2, mine, weight_part, 0)

    for k in range(4):
        for d in range(2):
            for h in range(2):
                bcopy(k, d, h).wait_recv()
        for h in range(2):
            hs = pl.ds(h * half, half)
            q[k, hs, :] += rb[k, 0, h].astype(f32) + rb[k, 1, h].astype(f32)
        if k < 3:
            sd[k] = q[k].astype(bf16)
            go(remote(sd.at[k], rd.at[z], d_send.at[k], d_recv.at[z], dev(order[k], 0, 0)))
    total = q[3]
    for k in range(3):
        zz = order[k]
        remote(sd.at[k], rd.at[zz], d_send.at[k], d_recv.at[zz], dev(zz, 0, 0)).wait_recv()
        total += rd[zz].astype(f32)
    hg_ref[...] = total.astype(bf16)

    for c in pending:
        c.wait_send()

    @pl.when(mid)
    def _():
        for c in pending_mid:
            c.wait_send()

    def stat_done(i, c):
        stat_copy(i).wait_send()
        return c
    lax.fori_loop(1, n, stat_done, 0)

    def out_done(j, c):
        pltpu.make_async_copy(wgs.at[j], wg_hbm.at[pl.ds(pl.multiple_of(j * width, width), width)],
                              out_sem.at[j]).wait()
        return c
    lax.fori_loop(0, mine, out_done, 0)


def fused(n, hidden, head_weight, mentor_outputs):
    tok, width = hidden.shape
    feats, voc = head_weight.shape
    half, mine = tok // 2, n // 2
    vm = pltpu.VMEM
    dma = pltpu.SemaphoreType.DMA
    anyspace = pl.BlockSpec(memory_space=pl.ANY)
    vspace = pl.BlockSpec(memory_space=pltpu.VMEM)
    hg, wg, mm = pl.pallas_call(
        stages,
        out_shape=(
            jax.ShapeDtypeStruct((tok, width), bf16),
            jax.ShapeDtypeStruct((feats // 2, voc), bf16),
            jax.ShapeDtypeStruct((1, tok), f32),
        ),
        in_specs=[anyspace] * 3,
        out_specs=(vspace, anyspace, vspace),
        scratch_shapes=[
            vm((n, tok, width), bf16),
            vm((mine, tok, width), bf16),
            vm((feats, voc), bf16),
            vm((tok, voc), bf16),
            vm((tok, voc), f32),
            vm((tok, voc), f32),
            vm((tok, voc), bf16),
            vm((tok, voc), bf16),
            vm((tok, 128), f32),
            vm((128, tok), f32),
            vm((n, 8, tok), f32),
            vm((4, 2, half, width), bf16),
            vm((4, 2, half, width), bf16),
            vm((4, 2, 2, half, width), bf16),
            vm((4, 2, 2, half, width), bf16),
            vm((4, 2, half, width), f32),
            vm((4, tok, width), f32),
            vm((3, tok, width), bf16),
            vm((4, tok, width), bf16),
            vm((mine, width, voc), bf16),
            dma((3,)),
            dma((n, 2)),
            dma((5, 2)),
            dma((4, 4)),
            dma((4, 2)),
            dma((n,)),
            dma((n,)),
            dma((4, 2)),
            dma((4, 2)),
            dma((4, 2, 2)),
            dma((4, 2, 2)),
            dma((3,)),
            dma((4,)),
            dma((2,)),
            dma((2,)),
            dma((mine,)),
        ],
        compiler_params=pltpu.CompilerParams(
            collective_id=0, has_side_effects=True, vmem_limit_bytes=48 * 1024 * 1024),
        cost_estimate=pl.CostEstimate(
            flops=6 * tok * feats * voc, transcendentals=2 * tok * voc,
            bytes_accessed=2 * feats * voc + feats * voc),
    )(hidden, head_weight, mentor_outputs)
    return hg, wg, mm.reshape(tok)


def collective(hidden, head_weight, mentor_outputs):
    full_hidden = lax.all_gather(hidden, "vocab", axis=1, tiled=True)
    student = jnp.dot(full_hidden, head_weight, preferred_element_type=f32) / sharpness_divisor
    target = mentor_outputs.astype(f32) / sharpness_divisor
    top_s, top_t = lax.pmax((jnp.max(student, axis=1), jnp.max(target, axis=1)), "vocab")
    exp_s = jnp.exp(student - top_s[:, None])
    exp_t = jnp.exp(target - top_t[:, None])
    total_s, total_t, weighted = lax.psum(
        (jnp.sum(exp_s, axis=1), jnp.sum(exp_t, axis=1),
         jnp.sum(exp_t * (target - student), axis=1)), "vocab")
    lse_s = top_s + jnp.log(total_s)
    lse_t = top_t + jnp.log(total_t)
    mismatch = sharpness_divisor * sharpness_divisor * (weighted / total_t + lse_s - lse_t)
    score = (objective_factor * sharpness_divisor
             * (jnp.exp(student - lse_s[:, None]) - jnp.exp(target - lse_t[:, None]))).astype(bf16)
    hidden_part = lax.psum_scatter(
        lax.dot_general(head_weight, score, NT, preferred_element_type=f32),
        "vocab", scatter_dimension=0, tiled=True)
    weight_grad = lax.psum_scatter(
        lax.dot_general(full_hidden, score, TN, preferred_element_type=f32),
        "rows", scatter_dimension=0, tiled=True).astype(bf16)
    return hidden_part.T.astype(bf16), weight_grad, mismatch


def solution(mesh):
    n = mesh.shape["vocab"]

    def shards(hidden, head_weight, mentor_outputs):
        if n == 16 and mesh.shape["rows"] == 2 and hidden.shape[1] % 128 == 0:
            return fused(n, hidden, head_weight, mentor_outputs)
        return collective(hidden, head_weight, mentor_outputs)

    return jax.shard_map(
        shards,
        mesh=mesh,
        in_specs=(P("rows", "vocab"), P(None, "vocab"), P("rows", "vocab")),
        out_specs=(P("rows", "vocab"), P("rows", "vocab"), P("rows")),
        check_vma=False,
    )
```

time: 310 us -> 63 us (0.20)
  waiting for transfers between devices: 180 us -> 0 us
  blocking collectives: 75.3 us -> 0 us
  Pallas kernels: 0 us -> 57 us
  matrix products: 24.3 us -> 0 us
  between operations: 13.8 us -> 0.65 us
  other arithmetic: 10 us -> 0 us
    reduce_scatter x2 -> x0, waiting for transfers between devices: 110 us -> none  [the longest x1 83 us: shards(): lax.psum_scatter(lax.dot_general(head_weight, raw_score_derivative, (((1,...]
    all_gather x1 -> x0, waiting for transfers between devices: 69.4 us -> none  [shards(): full_hidden = lax.all_gather(hidden, 'vocab', axis=1, tiled=True)]
    pallas_call x0 -> x1, Pallas kernels: none -> 57 us  [fused(): pl.pallas_call(stages, out_shape=(jax.ShapeDtypeStruct((tok, width), bf16...]
    pmax x1 -> x0, blocking collectives: 38.7 us -> none  [shards(): lax.pmax((jnp.max(learner_raw_outputs, axis=1), jnp.max(mentor_raw_output...]
    psum x1 -> x0, blocking collectives: 36.6 us -> none  [shards(): lax.psum((jnp.sum(exp_s, axis=1), jnp.sum(exp_t, axis=1), jnp.sum(exp_t *...]
    dot_general x3 -> x0, matrix products: 24.3 us -> none  [the longest x1 9.93 us: shards(): lax.dot_general(full_hidden, raw_score_derivative, (((0,), (0,)), ((), ()...]
    convert_element_type x2 -> x0, other arithmetic: 7.58 us -> none  [the longest x1 5.96 us: shards(): weight_grad = lax.psum_scatter(lax.dot_general(full_hidden, raw_score_der...]
    unnamed x3 -> x7, local copies, waits for them, and re-layouts: 6.39 us -> 5.17 us
  transfers between devices with their start and end apart: 3 -> 0, of which waited for: 3 -> 0; matrix products, arithmetic and copies ran while one was open for 4% -> 0% of each run, Pallas kernels for 0% -> 0%
where the time goes in v1:
time: 63 us; the launch traced here: 62.8 us
  Pallas kernels  57 us (90%)
  local copies, waits for them, and re-layouts  5.17 us (8%)
  between operations  0.65 us (1%)
    pallas_call x1, Pallas kernels, fused(): pl.pallas_call(stages, out_shape=(jax.ShapeDtypeStruct((tok, width), bf16...  57 us
    unnamed x7, local copies, waits for them, and re-layouts  5.17 us

profile of v1, /device:TPU:0, one launch (start us, length us, event | category | flops | bytes accessed | tf_op | source)
XLA Modules:
  0.0 62.8 jit_solution(4088364307480481036)
XLA Ops:
  0.6 0.0 copy-start
  0.6 1.0 %copy-done = bf16[256,1024]{1,0:T(8,128)(2,1)S(1)} copy-done((bf16[256,1024]{1,0:T(8,128)(2,1)S(1)}, bf16[256,1024]{1,0:T(8,128)(2,1)}, u32[]{:S(2)}) %copy-start) | copy-done | bytes 524312
  1.7 0.0 copy-start.1
  1.7 0.9 %copy-done.1 = bf16[256,256]{1,0:T(8,128)(2,1)S(1)} copy-done((bf16[256,256]{1,0:T(8,128)(2,1)S(1)}, bf16[256,256]{1,0:T(8,128)(2,1)}, u32[]{:S(2)}) %copy-start.1) | copy-done | bytes 131096
  2.6 57.0 %shard_map.58 = (bf16[256,256]{1,0:T(8,128)(2,1)S(1)}, bf16[2048,1024]{1,0:T(8,128)(2,1)S(1)}, f32[1,256]{1,0:T(1,128)S(1)}) custom-call(bf16[256,256]{1,0:T(8,128)(2,1)S(1)} %copy-done.1, bf16[4096,1024]{1,0:T(8,128)(2,1)} %w_hbm.1, bf16[256,1024]{1,0:T(8,128)(2,1)S(1)} %copy-done), custom_call_target="tpu_custom_call" | custom-call | flops 6442450944 | bytes 12582912 | tf_op jit(solution)/shard_map/pallas_call | solution.py:334
  59.6 0.7 %copy.9 = bf16[256,256]{1,0:T(8,128)(2,1)} copy(bf16[256,256]{1,0:T(8,128)(2,1)S(1)} %get-tuple-element.12) | data formatting | bytes 262144
  60.2 2.0 %copy.10 = bf16[2048,1024]{1,0:T(8,128)(2,1)} copy(bf16[2048,1024]{1,0:T(8,128)(2,1)S(1)} %get-tuple-element.13) | data formatting | bytes 8388608
  62.3 0.6 copy.11
Async XLA Ops:
  0.6 1.0 %copy-start = (bf16[256,1024]{1,0:T(8,128)(2,1)S(1)}, bf16[256,1024]{1,0:T(8,128)(2,1)}, u32[]{:S(2)}) copy-start(bf16[256,1024]{1,0:T(8,128)(2,1)} %t_hbm.1) | copy-start | bytes 1572868
  1.7 0.9 %copy-start.1 = (bf16[256,256]{1,0:T(8,128)(2,1)S(1)}, bf16[256,256]{1,0:T(8,128)(2,1)}, u32[]{:S(2)}) copy-start(bf16[256,256]{1,0:T(8,128)(2,1)} %h_hbm.1) | copy-start | bytes 393220

commit v2 on v1

v2 whole, which is shorter than its diff:
```python
import functools

import jax
import jax.numpy as jnp
from jax import lax
from jax.experimental import pallas as pl
from jax.experimental.pallas import tpu as pltpu
from jax.sharding import PartitionSpec as P

sharpness_divisor = 2.0
objective_factor = 32.0
f32 = jnp.float32
bf16 = jnp.bfloat16

NT = (((1,), (1,)), ((), ()))
TN = (((0,), (0,)), ((), ()))
BATCHES = 2


def stages(h_hbm, w_hbm, t_hbm, hg_ref, wg_hbm, mm_ref,
           gath, pgath, w, t, es, et, score, pscore, cols, rowsbuf, stat,
           sa, ra, sb, rb, pb, q, sd, rd, wgs,
           loc_sem, ag_recv, z_send, xy_send, f_send, st_send, st_recv,
           a_send, a_recv, b_send, b_recv, d_send, d_recv, p_send, p_recv, out_sem):
    n = gath.shape[0]
    tok, width = h_hbm.shape
    batch = tok // BATCHES
    half = batch // 2
    me = lax.axis_index("vocab")
    core = lax.axis_index("rows")
    z, y, x = me // 4, lax.rem(me // 2, 2), lax.rem(me, 2)
    mid = jnp.logical_or(z == 1, z == 2)

    def dev(zz, dy, dx):
        yy = 1 - y if dy else y
        xx = 1 - x if dx else x
        return zz * 4 + yy * 2 + xx

    z_near = z + 1 - 2 * lax.rem(z, 2)
    z_in = 3 - z
    low = z // 2
    planes = [z, z_near, 2 - low, 3 - 3 * low]
    order = planes[::-1]
    xdev, ydev = dev(z, 0, 1), dev(z, 1, 0)
    zn_dev, zi_dev = dev(z_near, 0, 0), dev(z_in, 0, 0)

    def remote(src, dst, ss, rs, target):
        return pltpu.make_async_remote_copy(
            src_ref=src, dst_ref=dst, send_sem=ss, recv_sem=rs,
            device_id={"vocab": target}, device_id_type=pl.DeviceIdType.MESH)

    def partner(src, dst, i):
        return pltpu.make_async_remote_copy(
            src_ref=src, dst_ref=dst, send_sem=p_send.at[i], recv_sem=p_recv.at[i],
            device_id={"rows": 1 - core}, device_id_type=pl.DeviceIdType.MESH)

    cp_h = pltpu.make_async_copy(h_hbm, gath.at[me], loc_sem.at[0])
    cp_w = pltpu.make_async_copy(w_hbm, w, loc_sem.at[1])
    cp_t = pltpu.make_async_copy(t_hbm, t, loc_sem.at[2])
    cp_h.start()
    cp_t.start()
    cp_w.start()

    barrier = pltpu.get_barrier_semaphore()

    def greet(i, c):
        pl.semaphore_signal(barrier, inc=1, device_id={"vocab": lax.rem(me + i, n)},
                            device_id_type=pl.DeviceIdType.MESH)
        return c
    lax.fori_loop(1, n, greet, 0)
    pl.semaphore_signal(barrier, inc=1, device_id={"rows": 1 - core},
                        device_id_type=pl.DeviceIdType.MESH)
    pl.semaphore_wait(barrier, n)
    cp_h.wait()

    pending, pending_mid = [], []

    def go(c):
        c.start()
        pending.append(c)

    def go_mid(c):
        pl.when(mid)(c.start)
        pending_mid.append(c)

    def gcopy(b, slot, h, ss, target):
        ref = gath.at[slot, pl.ds(b * batch + h * half, half)]
        return remote(ref, ref, ss, ag_recv.at[slot, b, h], target)

    def wait_piece(b, slot, h):
        gcopy(b, slot, h, f_send.at[b, 0, 0], xdev).wait_recv()

    def z_start(b):
        for h in range(2):
            go(gcopy(b, me, h, z_send.at[b, 0, h], zn_dev))
            go_mid(gcopy(b, me, h, z_send.at[b, 1, h], zi_dev))

    def z_step(b, i):
        slot = dev(planes[i], 0, 0)
        for h in range(2):
            wait_piece(b, slot, h)
            go_mid(gcopy(b, slot, h, z_send.at[b, 1 + i, h], zi_dev if i == 1 else zn_dev))

    def fan_out(b, i):
        slot = dev(planes[i], 0, 0)
        go(gcopy(b, slot, 0, xy_send.at[b, i, 0], ydev))
        go(gcopy(b, slot, 1, xy_send.at[b, i, 1], xdev))
        go(gcopy(b, slot, 1, xy_send.at[b, i, 2], ydev))
        go(gcopy(b, slot, 0, xy_send.at[b, i, 3], xdev))

    def forward(b, i):
        s0, s1 = dev(planes[i], 1, 0), dev(planes[i], 0, 1)
        wait_piece(b, s0, 0)
        go(gcopy(b, s0, 0, f_send.at[b, i, 0], xdev))
        wait_piece(b, s1, 1)
        go(gcopy(b, s1, 1, f_send.at[b, i, 1], ydev))

    def wrows(slot):
        return pl.ds(pl.multiple_of(slot * width, width), width)

    def brows(b):
        return pl.ds(b * batch, batch)

    def multiply(b, slot, first=False):
        part = jnp.dot(gath[slot, brows(b), :], w[wrows(slot), :], preferred_element_type=f32)
        if first:
            es[brows(b), :] = part
        else:
            es[brows(b), :] += part

    def sides(b, i):
        s0, s1 = dev(planes[i], 1, 0), dev(planes[i], 0, 1)
        wait_piece(b, s0, 1)
        multiply(b, s0)
        wait_piece(b, s1, 0)
        multiply(b, s1)

    def diagonal(b, i):
        s = dev(planes[i], 1, 1)
        wait_piece(b, s, 0)
        wait_piece(b, s, 1)
        multiply(b, s)

    block = 32
    nblk = batch // block
    lane = lax.broadcasted_iota(jnp.int32, (block, 128), 1)

    def teacher(i, c):
        rows = pl.ds(pl.multiple_of(i * block, block), block)
        tv = t[rows, :].astype(f32) / sharpness_divisor
        m = jnp.max(tv, axis=1, keepdims=True)
        e = jnp.exp(tv - m)
        et[rows, :] = e
        total = jnp.sum(e, axis=1, keepdims=True)
        cols[rows, :] = jnp.where(lane == 2, m, jnp.where(lane == 3, total, 0.0))
        return c

    def student(i, c):
        rows = pl.ds(pl.multiple_of(i * block, block), block)
        sv = es[rows, :] / sharpness_divisor
        tv = t[rows, :].astype(f32) / sharpness_divisor
        m = jnp.max(sv, axis=1, keepdims=True)
        e = jnp.exp(sv - m)
        es[rows, :] = e
        total = jnp.sum(e, axis=1, keepdims=True)
        weighted = jnp.sum(et[rows, :] * (tv - sv), axis=1, keepdims=True)
        old = cols[rows, :]
        cols[rows, :] = jnp.where(
            lane == 0, m, jnp.where(lane == 1, total, jnp.where(lane == 4, weighted, old)))
        return c

    def stat_copy(b, i):
        return remote(stat.at[b, me], stat.at[b, me], st_send.at[b, i], st_recv.at[b, me],
                      lax.rem(me + i, n))

    def stat_send(b):
        lax.fori_loop(b * nblk, (b + 1) * nblk, student, 0)
        stat[b, me] = jnp.transpose(cols[brows(b), :])[:8, :]

        def start(i, c):
            stat_copy(b, i).start()
            return c
        lax.fori_loop(1, n, start, 0)

    def derive(i, c):
        rows = pl.ds(pl.multiple_of(i * block, block), block)
        f = cols[rows, :]
        score[rows, :] = (es[rows, :] * f[:, 0:1] - et[rows, :] * f[:, 1:2]).astype(bf16)
        return c

    def stat_join(b):
        def wait(i, c):
            other = lax.rem(me + i, n)
            remote(stat.at[b, other], stat.at[b, other], st_send.at[b, i],
                   st_recv.at[b, other], other).wait_recv()
            return c
        lax.fori_loop(1, n, wait, 0)
        ms, ss = stat[b, :, 0:1, :], stat[b, :, 1:2, :]
        mt, tt, wt = stat[b, :, 2:3, :], stat[b, :, 3:4, :], stat[b, :, 4:5, :]
        top_s, top_t = jnp.max(ms, axis=0), jnp.max(mt, axis=0)
        total_s = jnp.sum(ss * jnp.exp(ms - top_s[None]), axis=0)
        scale_t = jnp.exp(mt - top_t[None])
        total_t = jnp.sum(tt * scale_t, axis=0)
        cross = jnp.sum(wt * scale_t, axis=0) / total_t
        lse_s = top_s + jnp.log(total_s)
        lse_t = top_t + jnp.log(total_t)
        mm_ref[:, brows(b)] = sharpness_divisor * sharpness_divisor * (cross + lse_s - lse_t)
        own = stat[b, me]
        gain = objective_factor * sharpness_divisor
        rowsbuf[b, 0:1, :] = gain * jnp.exp(own[0:1, :] - lse_s)
        rowsbuf[b, 1:2, :] = gain * jnp.exp(own[2:3, :] - lse_t)
        cols[brows(b), :] = jnp.transpose(rowsbuf[b])
        lax.fori_loop(b * nblk, (b + 1) * nblk, derive, 0)

    def part(b, slot):
        return lax.dot_general(score[brows(b), :], w[wrows(slot), :], NT,
                               preferred_element_type=f32)

    def acopy(b, k, h):
        return remote(sa.at[b, k, h], ra.at[b, k, h], a_send.at[b, k, h],
                      a_recv.at[b, k, h], ydev if h else xdev)

    def bcopy(b, k, d, h):
        return remote(sb.at[b, k, d, h], rb.at[b, k, d, h], b_send.at[b, k, d, h],
                      b_recv.at[b, k, d, h], xdev if d else ydev)

    def spread(b):
        for k in range(4):
            p = part(b, dev(order[k], 1, 1)).astype(bf16)
            sa[b, k, 0] = p[:half]
            sa[b, k, 1] = p[half:]
            go(acopy(b, k, 0))
            go(acopy(b, k, 1))
        for k in range(4):
            p = part(b, dev(order[k], 1, 0))
            pb[b, k, 0] = p[:half]
            sb[b, k, 0, 1] = p[half:].astype(bf16)
            go(bcopy(b, k, 0, 1))
            p = part(b, dev(order[k], 0, 1))
            pb[b, k, 1] = p[half:]
            sb[b, k, 1, 0] = p[:half].astype(bf16)
            go(bcopy(b, k, 1, 0))

    def home(b):
        for k in range(4):
            q[b, k] = part(b, dev(order[k], 0, 0))

    def join(b, k):
        acopy(b, k, 0).wait_recv()
        sb[b, k, 0, 0] = (pb[b, k, 0] + ra[b, k, 0].astype(f32)).astype(bf16)
        go(bcopy(b, k, 0, 0))
        acopy(b, k, 1).wait_recv()
        sb[b, k, 1, 1] = (pb[b, k, 1] + ra[b, k, 1].astype(f32)).astype(bf16)
        go(bcopy(b, k, 1, 1))

    def column(b, k):
        for d in range(2):
            for h in range(2):
                bcopy(b, k, d, h).wait_recv()
        for h in range(2):
            hs = pl.ds(h * half, half)
            q[b, k, hs, :] += rb[b, k, 0, h].astype(f32) + rb[b, k, 1, h].astype(f32)
        if k < 3:
            sd[b, k] = q[b, k].astype(bf16)
            go(remote(sd.at[b, k], rd.at[b, z], d_send.at[b, k], d_recv.at[b, z],
                      dev(order[k], 0, 0)))

    def finish(b):
        total = q[b, 3]
        for k in range(3):
            zz = order[k]
            remote(sd.at[b, k], rd.at[b, zz], d_send.at[b, k], d_recv.at[b, zz],
                   dev(zz, 0, 0)).wait_recv()
            total += rd[b, zz].astype(f32)
        hg_ref[brows(b), :] = total.astype(bf16)

    mine = n // 2

    def out_copy(j):
        return pltpu.make_async_copy(
            wgs.at[j], wg_hbm.at[pl.ds(pl.multiple_of(j * width, width), width)], out_sem.at[j])

    def weight_part(j, c):
        slot = core * mine + j
        for v in range(2):
            vs = pl.ds(v * (w.shape[1] // 2), w.shape[1] // 2)
            g = lax.dot_general(gath[slot], score[:, vs], TN, preferred_element_type=f32)
            g += lax.dot_general(pgath[j], pscore[:, vs], TN, preferred_element_type=f32)
            wgs[j, :, vs] = g.astype(bf16)
        out_copy(j).start()
        return c

    z_start(0)
    fan_out(0, 0)
    z_start(1)
    rowsbuf[...] = jnp.zeros_like(rowsbuf)
    cp_t.wait()
    lax.fori_loop(0, BATCHES * nblk, teacher, 0)
    cp_w.wait()
    multiply(0, me, True)
    for i in range(1, 4):
        z_step(0, i)
        fan_out(0, i)
        z_step(1, i)
        forward(0, i - 1)
        multiply(0, dev(planes[i], 0, 0))
        if i > 1:
            sides(0, i - 2)
    forward(0, 3)
    for i in range(4):
        fan_out(1, i)
    diagonal(0, 0)
    diagonal(0, 1)
    forward(1, 0)
    sides(0, 2)
    diagonal(0, 2)
    sides(0, 3)
    diagonal(0, 3)
    stat_send(0)
    forward(1, 1)
    multiply(1, me, True)
    multiply(1, dev(planes[1], 0, 0))
    sides(1, 0)
    forward(1, 2)
    stat_join(0)
    forward(1, 3)
    spread(0)
    multiply(1, dev(planes[2], 0, 0))
    multiply(1, dev(planes[3], 0, 0))
    for i in range(4):
        if i:
            sides(1, i)
        diagonal(1, i)
    ph = partner(gath.at[pl.ds((1 - core) * mine, mine)], pgath, 0)
    ph.start()
    stat_send(1)
    for k in range(4):
        join(0, k)
    home(0)
    stat_join(1)
    ps = partner(score, pscore, 1)
    ps.start()
    spread(1)
    for k in range(4):
        column(0, k)
    home(1)
    join(1, 0)
    join(1, 1)
    ph.wait()
    ps.wait()
    lax.fori_loop(0, mine // 2, weight_part, 0)
    join(1, 2)
    join(1, 3)
    finish(0)
    lax.fori_loop(mine // 2, mine, weight_part, 0)
    for k in range(4):
        column(1, k)
    finish(1)

    for c in pending:
        c.wait_send()

    @pl.when(mid)
    def _():
        for c in pending_mid:
            c.wait_send()

    def stat_done(i, c):
        for b in range(BATCHES):
            stat_copy(b, i).wait_send()
        return c
    lax.fori_loop(1, n, stat_done, 0)

    def out_done(j, c):
        out_copy(j).wait()
        return c
    lax.fori_loop(0, mine, out_done, 0)


def publish(*refs):
    k = len(refs) // 2
    sems = refs[-1]
    copies = [pltpu.make_async_copy(refs[i], refs[k + i], sems.at[i]) for i in range(k)]
    for c in copies:
        c.start()
    for c in copies:
        c.wait()


def fused(n, hidden, head_weight, mentor_outputs):
    tok, width = hidden.shape
    feats, voc = head_weight.shape
    batch, mine = tok // BATCHES, n // 2
    half = batch // 2
    nb = BATCHES
    vm = pltpu.VMEM
    dma = pltpu.SemaphoreType.DMA
    anyspace = pl.BlockSpec(memory_space=pl.ANY)
    vspace = pl.BlockSpec(memory_space=pltpu.VMEM)
    hbm = pl.BlockSpec(memory_space=pltpu.HBM)
    shapes = (
        jax.ShapeDtypeStruct((tok, width), bf16),
        jax.ShapeDtypeStruct((feats // 2, voc), bf16),
        jax.ShapeDtypeStruct((1, tok), f32),
    )
    made = pl.pallas_call(
        stages,
        out_shape=shapes,
        in_specs=[hbm] * 3,
        out_specs=(vspace, anyspace, vspace),
        scratch_shapes=[
            vm((n, tok, width), bf16),
            vm((mine, tok, width), bf16),
            vm((feats, voc), bf16),
            vm((tok, voc), bf16),
            vm((tok, voc), f32),
            vm((tok, voc), f32),
            vm((tok, voc), bf16),
            vm((tok, voc), bf16),
            vm((tok, 128), f32),
            vm((nb, 128, batch), f32),
            vm((nb, n, 8, batch), f32),
            vm((nb, 4, 2, half, width), bf16),
            vm((nb, 4, 2, half, width), bf16),
            vm((nb, 4, 2, 2, half, width), bf16),
            vm((nb, 4, 2, 2, half, width), bf16),
            vm((nb, 4, 2, half, width), f32),
            vm((nb, 4, batch, width), f32),
            vm((nb, 3, batch, width), bf16),
            vm((nb, 4, batch, width), bf16),
            vm((mine, width, voc), bf16),
            dma((3,)),
            dma((n, nb, 2)),
            dma((nb, 5, 2)),
            dma((nb, 4, 4)),
            dma((nb, 4, 2)),
            dma((nb, n)),
            dma((nb, n)),
            dma((nb, 4, 2)),
            dma((nb, 4, 2)),
            dma((nb, 4, 2, 2)),
            dma((nb, 4, 2, 2)),
            dma((nb, 3)),
            dma((nb, 4)),
            dma((2,)),
            dma((2,)),
            dma((mine,)),
        ],
        compiler_params=pltpu.CompilerParams(
            collective_id=0, has_side_effects=True, vmem_limit_bytes=48 * 1024 * 1024),
        cost_estimate=pl.CostEstimate(
            flops=6 * tok * feats * voc, transcendentals=2 * tok * voc,
            bytes_accessed=2 * feats * voc + feats * voc),
    )(hidden, head_weight, mentor_outputs)
    hg, wg, mm = pl.pallas_call(
        publish,
        out_shape=shapes,
        in_specs=[anyspace] * 3,
        out_specs=(hbm,) * 3,
        scratch_shapes=[dma((3,))],
    )(*made)
    return hg, wg, mm.reshape(tok)


def collective(hidden, head_weight, mentor_outputs):
    full_hidden = lax.all_gather(hidden, "vocab", axis=1, tiled=True)
    student = jnp.dot(full_hidden, head_weight, preferred_element_type=f32) / sharpness_divisor
    target = mentor_outputs.astype(f32) / sharpness_divisor
    top_s, top_t = lax.pmax((jnp.max(student, axis=1), jnp.max(target, axis=1)), "vocab")
    exp_s = jnp.exp(student - top_s[:, None])
    exp_t = jnp.exp(target - top_t[:, None])
    total_s, total_t, weighted = lax.psum(
        (jnp.sum(exp_s, axis=1), jnp.sum(exp_t, axis=1),
         jnp.sum(exp_t * (target - student), axis=1)), "vocab")
    lse_s = top_s + jnp.log(total_s)
    lse_t = top_t + jnp.log(total_t)
    mismatch = sharpness_divisor * sharpness_divisor * (weighted / total_t + lse_s - lse_t)
    score = (objective_factor * sharpness_divisor
             * (jnp.exp(student - lse_s[:, None]) - jnp.exp(target - lse_t[:, None]))).astype(bf16)
    hidden_part = lax.psum_scatter(
        lax.dot_general(head_weight, score, NT, preferred_element_type=f32),
        "vocab", scatter_dimension=0, tiled=True)
    weight_grad = lax.psum_scatter(
        lax.dot_general(full_hidden, score, TN, preferred_element_type=f32),
        "rows", scatter_dimension=0, tiled=True).astype(bf16)
    return hidden_part.T.astype(bf16), weight_grad, mismatch


def solution(mesh):
    n = mesh.shape["vocab"]

    def shards(hidden, head_weight, mentor_outputs):
        if n == 16 and mesh.shape["rows"] == 2 and hidden.shape[1] % 128 == 0:
            return fused(n, hidden, head_weight, mentor_outputs)
        return collective(hidden, head_weight, mentor_outputs)

    return jax.shard_map(
        shards,
        mesh=mesh,
        in_specs=(P("rows", "vocab"), P(None, "vocab"), P("rows", "vocab")),
        out_specs=(P("rows", "vocab"), P("rows", "vocab"), P("rows")),
        check_vma=False,
    )
```

time: 63 us -> 204 us (3.24)
  Pallas kernels: 57 us -> 198 us
    pallas_call x1 -> x2, Pallas kernels: 57 us -> 198 us  [the longest x1 132 us: fused(): pl.pallas_call(publish, out_shape=shapes, in_specs=[anyspace] * 3, out_sp...]
    unnamed x7 -> x10, local copies, waits for them, and re-layouts: 5.17 us -> 5.09 us
where the time goes in v2:
time: 204 us
  Pallas kernels  198 us (97%)
  local copies, waits for them, and re-layouts  5.09 us (2%)
    pallas_call x1, Pallas kernels, fused(): pl.pallas_call(publish, out_shape=shapes, in_specs=[anyspace] * 3, out_sp...  132 us
    pallas_call x1, Pallas kernels, fused(): pl.pallas_call(stages, out_shape=shapes, in_specs=[hbm] * 3, out_specs=(v...  65.8 us
    unnamed x10, local copies, waits for them, and re-layouts  5.09 us

profile of v2, /device:TPU:0, one launch (start us, length us, event | category | flops | bytes accessed | tf_op | source)
XLA Modules:
  0.0 203.7 jit_solution(11609612025986337105)
XLA Ops:
  0.6 0.0 copy-start.3
  0.6 1.0 copy-done.3
  1.7 0.0 copy-start.4
  1.7 0.9 copy-done.4
  2.6 65.8 %shard_map.58 = (bf16[256,256]{1,0:T(8,128)(2,1)S(1)}, bf16[2048,1024]{1,0:T(8,128)(2,1)S(1)}, f32[1,256]{1,0:T(1,128)S(1)}) custom-call(bf16[256,256]{1,0:T(8,128)(2,1)S(1)} %copy-done.4, bf16[4096,1024]{1,0:T(8,128)(2,1)} %w_hbm.1, bf16[256,1024]{1,0:T(8,128)(2,1)S(1)} %copy-done.3), custom_call_target="tpu_custom_call" | custom-call | flops 6442450944 | bytes 12582912 | tf_op jit(solution)/shard_map/pallas_call | solution.py:406
  68.4 0.0 copy-start
  68.4 1.9 copy-done
  70.3 0.0 copy-start.1
  70.3 0.6 copy-done.1
  70.9 0.0 copy-start.2
  70.9 0.6 copy-done.2
  71.5 132.2 %shard_map.59 = (bf16[256,256]{1,0:T(8,128)(2,1)}, bf16[2048,1024]{1,0:T(8,128)(2,1)}, f32[1,256]{1,0:T(1,128)}) custom-call(bf16[256,256]{1,0:T(8,128)(2,1)} %copy-done.1, bf16[2048,1024]{1,0:T(8,128)(2,1)} %copy-done, f32[1,256]{1,0:T(1,128)} %copy-done.2), custom_call_target="tpu_custom_call" | custom-call | tf_op jit(solution)/shard_map/pallas_call | solution.py:455
Async XLA Ops:
  0.6 1.0 copy-start.3
  1.7 0.9 copy-start.4
  68.4 1.9 copy-start
  70.3 0.6 copy-start.1
  70.9 0.6 copy-start.2

commit v3 on v1

--- a/solution.py
+++ b/solution.py
@@ -16,13 +16,13 @@
 TN = (((0,), (0,)), ((), ()))
 
 
-def stages(h_hbm, w_hbm, t_hbm, hg_ref, wg_hbm, mm_ref,
-           gath, pgath, w, t, es, et, score, pscore, cols, rowsbuf, stat,
-           sa, ra, sb, rb, pb, q, sd, rd, wgs,
+def stages(h_ref, w_hbm, t, hg_ref, wg_ref, mm_ref,
+           gath, pgath, w, es, et, score, cols, rowsbuf, stat,
+           sa, ra, sb, rb, pp, sd, rd,
            loc_sem, ag_recv, z_send, xy_send, f_send, st_send, st_recv,
-           a_send, a_recv, b_send, b_recv, d_send, d_recv, p_send, p_recv, out_sem):
+           a_send, a_recv, b_send, b_recv, d_send, d_recv, p_send, p_recv):
     n = gath.shape[0]
-    tok, width = h_hbm.shape
+    tok, width = h_ref.shape
     half = tok // 2
     me = lax.axis_index("vocab")
     core = lax.axis_index("rows")
@@ -50,12 +50,9 @@
             src_ref=src, dst_ref=dst, send_sem=p_send.at[i], recv_sem=p_recv.at[i],
             device_id={"rows": 1 - core}, device_id_type=pl.DeviceIdType.MESH)
 
-    cp_h = pltpu.make_async_copy(h_hbm, gath.at[me], loc_sem.at[0])
-    cp_w = pltpu.make_async_copy(w_hbm, w, loc_sem.at[1])
-    cp_t = pltpu.make_async_copy(t_hbm, t, loc_sem.at[2])
-    cp_h.start()
-    cp_t.start()
+    cp_w = pltpu.make_async_copy(w_hbm, w, loc_sem.at[0])
     cp_w.start()
+    gath[me] = h_ref[...]
 
     barrier = pltpu.get_barrier_semaphore()
 
@@ -67,7 +64,6 @@
     pl.semaphore_signal(barrier, inc=1, device_id={"rows": 1 - core},
                         device_id_type=pl.DeviceIdType.MESH)
     pl.semaphore_wait(barrier, n)
-    cp_h.wait()
 
     def piece(slot, h):
         return gath.at[slot, pl.ds(h * half, half)]
@@ -102,15 +98,29 @@
         wait_piece(s1, 1)
         go(gcopy(s1, 1, f_send.at[i, 1], ydev))
 
-    def wrows(slot):
-        return pl.ds(pl.multiple_of(slot * width, width), width)
-
-    def multiply(slot, first=False):
-        part = jnp.dot(gath[slot], w[wrows(slot), :], preferred_element_type=f32)
+    def wrows(slot, count):
+        return pl.ds(pl.multiple_of(slot * width, width), count * width)
+
+    def multiply(slot, count, first=False):
+        a = jnp.concatenate([gath[slot + c] for c in range(count)], axis=1)
+        part = jnp.dot(a, w[wrows(slot, count), :], preferred_element_type=f32)
         if first:
             es[...] = part
         else:
             es[...] += part
+
+    def plane(i):
+        s0, s1, s = dev(planes[i], 1, 0), dev(planes[i], 0, 1), dev(planes[i], 1, 1)
+        wait_piece(s0, 1)
+        wait_piece(s1, 0)
+        if i == 3:
+            multiply(planes[3] * 4 + 2 * y, 2)
+        wait_piece(s, 0)
+        wait_piece(s, 1)
+        if i == 3:
+            multiply(planes[3] * 4 + 2 * (1 - y), 2)
+        else:
+            multiply(planes[i] * 4, 4, i == 0)
 
     zn_dev, zi_dev = dev(z_near, 0, 0), dev(z_in, 0, 0)
     for h in range(2):
@@ -121,7 +131,6 @@
     block = 32
     nblk = tok // block
     lane = lax.broadcasted_iota(jnp.int32, (block, 128), 1)
-    cp_t.wait()
 
     def teacher(b, c):
         rows = pl.ds(pl.multiple_of(b * block, block), block)
@@ -134,8 +143,6 @@
         return c
     lax.fori_loop(0, nblk, teacher, 0)
 
-    cp_w.wait()
-    multiply(me, True)
     for i in range(1, 4):
         slot = dev(planes[i], 0, 0)
         target = zi_dev if i == 1 else zn_dev
@@ -144,28 +151,13 @@
             go_mid(gcopy(slot, h, z_send.at[1 + i, h], target))
         fan_out(i)
         forward(i - 1)
-        multiply(slot)
         if i > 1:
-            s0, s1 = dev(planes[i - 2], 1, 0), dev(planes[i - 2], 0, 1)
-            wait_piece(s0, 1)
-            multiply(s0)
-            wait_piece(s1, 0)
-            multiply(s1)
+            if i == 2:
+                cp_w.wait()
+            plane(i - 2)
     forward(3)
-    for i in range(2):
-        s = dev(planes[i], 1, 1)
-        wait_piece(s, 0)
-        wait_piece(s, 1)
-        multiply(s)
-    for i in range(2, 4):
-        s0, s1, s = dev(planes[i], 1, 0), dev(planes[i], 0, 1), dev(planes[i], 1, 1)
-        wait_piece(s0, 1)
-        multiply(s0)
-        wait_piece(s1, 0)
-        multiply(s1)
-        wait_piece(s, 0)
-        wait_piece(s, 1)
-        multiply(s)
+    plane(2)
+    plane(3)
 
     mine = n // 2
     ph = partner(gath.at[pl.ds((1 - core) * mine, mine)], pgath, 0)
@@ -226,77 +218,77 @@
         score[rows, :] = (es[rows, :] * f[:, 0:1] - et[rows, :] * f[:, 1:2]).astype(bf16)
         return c
     lax.fori_loop(0, nblk, derive, 0)
-    ps = partner(score, pscore, 1)
+    ps = partner(score.at[pl.ds(0, tok)], score.at[pl.ds(tok, tok)], 1)
     ps.start()
 
-    def part(slot):
-        return lax.dot_general(score[...], w[wrows(slot), :], NT, preferred_element_type=f32)
-
     order = [planes[3], planes[2], planes[1], planes[0]]
-    for k in range(4):
-        p = part(dev(order[k], 1, 1)).astype(bf16)
-        sa[k, 0] = p[:half]
-        sa[k, 1] = p[half:]
-        go(remote(sa.at[k, 0], ra.at[k, 0], a_send.at[k, 0], a_recv.at[k, 0], xdev))
-        go(remote(sa.at[k, 1], ra.at[k, 1], a_send.at[k, 1], a_recv.at[k, 1], ydev))
+
+    def block_of(dy, dx):
+        slot = dev(0, dy, dx)
+        return pl.ds(pl.multiple_of(slot * width, width), width)
+
+    near, beside, across, diag = block_of(0, 0), block_of(1, 0), block_of(0, 1), block_of(1, 1)
+    top, bottom = pl.ds(0, half), pl.ds(half, half)
 
     def bcopy(k, d, h):
         return remote(sb.at[k, d, h], rb.at[k, d, h], b_send.at[k, d, h],
                       b_recv.at[k, d, h], xdev if d else ydev)
 
     for k in range(4):
-        p = part(dev(order[k], 1, 0))
-        pb[k, 0] = p[:half]
-        sb[k, 0, 1] = p[half:].astype(bf16)
+        pp[k] = lax.dot_general(score[:tok, :], w[wrows(order[k] * 4, 4), :], NT,
+                                preferred_element_type=f32)
+        sa[k, 0] = pp[k, top, diag].astype(bf16)
+        sa[k, 1] = pp[k, bottom, diag].astype(bf16)
+        go(remote(sa.at[k, 0], ra.at[k, 0], a_send.at[k, 0], a_recv.at[k, 0], xdev))
+        go(remote(sa.at[k, 1], ra.at[k, 1], a_send.at[k, 1], a_recv.at[k, 1], ydev))
+        sb[k, 0, 1] = pp[k, bottom, beside].astype(bf16)
         go(bcopy(k, 0, 1))
-        p = part(dev(order[k], 0, 1))
-        pb[k, 1] = p[half:]
-        sb[k, 1, 0] = p[:half].astype(bf16)
+        sb[k, 1, 0] = pp[k, top, across].astype(bf16)
         go(bcopy(k, 1, 0))
-    for k in range(4):
-        q[k] = part(dev(order[k], 0, 0))
+
+    pair = 2
 
     def weight_part(j, c):
-        slot = core * mine + j
+        slot = core * mine + j * pair
+        a = jnp.concatenate(
+            [jnp.concatenate([gath[slot + i], pgath[j * pair + i]], axis=0) for i in range(pair)],
+            axis=1)
         for v in range(2):
             vs = pl.ds(v * (w.shape[1] // 2), w.shape[1] // 2)
-            g = lax.dot_general(gath[slot], score[:, vs], TN, preferred_element_type=f32)
-            g += lax.dot_general(pgath[j], pscore[:, vs], TN, preferred_element_type=f32)
-            wgs[j, :, vs] = g.astype(bf16)
-        pltpu.make_async_copy(wgs.at[j], wg_hbm.at[pl.ds(pl.multiple_of(j * width, width), width)],
-                              out_sem.at[j]).start()
+            g = lax.dot_general(a, score[:, vs], TN, preferred_element_type=f32)
+            wg_ref[pl.ds(pl.multiple_of(j * pair * width, width), pair * width), vs] = g.astype(bf16)
         return c
 
     def join(k):
         a = remote(sa.at[k, 0], ra.at[k, 0], a_send.at[k, 0], a_recv.at[k, 0], xdev)
         a.wait_recv()
-        sb[k, 0, 0] = (pb[k, 0] + ra[k, 0].astype(f32)).astype(bf16)
+        sb[k, 0, 0] = (pp[k, top, beside] + ra[k, 0].astype(f32)).astype(bf16)
         go(bcopy(k, 0, 0))
         a = remote(sa.at[k, 1], ra.at[k, 1], a_send.at[k, 1], a_recv.at[k, 1], ydev)
         a.wait_recv()
-        sb[k, 1, 1] = (pb[k, 1] + ra[k, 1].astype(f32)).astype(bf16)
+        sb[k, 1, 1] = (pp[k, bottom, across] + ra[k, 1].astype(f32)).astype(bf16)
         go(bcopy(k, 1, 1))
 
     join(0)
     join(1)
     ph.wait()
     ps.wait()
-    lax.fori_loop(0, mine // 2, weight_part, 0)
+    lax.fori_loop(0, mine // (2 * pair), weight_part, 0)
     join(2)
     join(3)
-    lax.fori_loop(mine // 2, mine, weight_part, 0)
+    lax.fori_loop(mine // (2 * pair), mine // pair, weight_part, 0)
 
     for k in range(4):
         for d in range(2):
             for h in range(2):
                 bcopy(k, d, h).wait_recv()
         for h in range(2):
-            hs = pl.ds(h * half, half)
-            q[k, hs, :] += rb[k, 0, h].astype(f32) + rb[k, 1, h].astype(f32)
+            hs = bottom if h else top
+            pp[k, hs, near] += rb[k, 0, h].astype(f32) + rb[k, 1, h].astype(f32)
         if k < 3:
-            sd[k] = q[k].astype(bf16)
+            sd[k] = pp[k, :, near].astype(bf16)
             go(remote(sd.at[k], rd.at[z], d_send.at[k], d_recv.at[z], dev(order[k], 0, 0)))
-    total = q[3]
+    total = pp[3, :, near]
     for k in range(3):
         zz = order[k]
         remote(sd.at[k], rd.at[zz], d_send.at[k], d_recv.at[zz], dev(zz, 0, 0)).wait_recv()
@@ -315,13 +307,6 @@
         stat_copy(i).wait_send()
         return c
     lax.fori_loop(1, n, stat_done, 0)
-
-    def out_done(j, c):
-        pltpu.make_async_copy(wgs.at[j], wg_hbm.at[pl.ds(pl.multiple_of(j * width, width), width)],
-                              out_sem.at[j]).wait()
-        return c
-    lax.fori_loop(0, mine, out_done, 0)
-
 
 def fused(n, hidden, head_weight, mentor_outputs):
     tok, width = hidden.shape
@@ -338,17 +323,15 @@
             jax.ShapeDtypeStruct((feats // 2, voc), bf16),
             jax.ShapeDtypeStruct((1, tok), f32),
         ),
-        in_specs=[anyspace] * 3,
-        out_specs=(vspace, anyspace, vspace),
+        in_specs=[vspace, anyspace, vspace],
+        out_specs=(vspace,) * 3,
         scratch_shapes=[
             vm((n, tok, width), bf16),
             vm((mine, tok, width), bf16),
             vm((feats, voc), bf16),
-            vm((tok, voc), bf16),
             vm((tok, voc), f32),
             vm((tok, voc), f32),
-            vm((tok, voc), bf16),
-            vm((tok, voc), bf16),
+            vm((2 * tok, voc), bf16),
             vm((tok, 128), f32),
             vm((128, tok), f32),
             vm((n, 8, tok), f32),
@@ -356,12 +339,10 @@
             vm((4, 2, half, width), bf16),
             vm((4, 2, 2, half, width), bf16),
             vm((4, 2, 2, half, width), bf16),
-            vm((4, 2, half, width), f32),
-            vm((4, tok, width), f32),
+            vm((4, tok, 4 * width), f32),
             vm((3, tok, width), bf16),
             vm((4, tok, width), bf16),
-            vm((mine, width, voc), bf16),
-            dma((3,)),
+            dma((1,)),
             dma((n, 2)),
             dma((5, 2)),
             dma((4, 4)),
@@ -376,7 +357,6 @@
             dma((4,)),
             dma((2,)),
             dma((2,)),
-            dma((mine,)),
         ],
         compiler_params=pltpu.CompilerParams(
             collective_id=0, has_side_effects=True, vmem_limit_bytes=48 * 1024 * 1024),

time: 63 us -> 63.6 us (level)
  no operation moved by 1% of the time
where the time goes in v3:
time: 63.6 us; the launch traced here: 63.4 us
  Pallas kernels  57.6 us (91%)
  local copies, waits for them, and re-layouts  5.17 us (8%)
  between operations  0.65 us (1%)
    pallas_call x1, Pallas kernels, fused(): pl.pallas_call(stages, out_shape=(jax.ShapeDtypeStruct((tok, width), bf16...  57.6 us
    unnamed x7, local copies, waits for them, and re-layouts  5.17 us

profile of v3, /device:TPU:0, one launch (start us, length us, event | category | flops | bytes accessed | tf_op | source)
XLA Modules:
  0.0 63.4 jit_solution(7837005629692546829)
XLA Ops:
  0.6 0.0 copy-start
  0.6 1.0 %copy-done = bf16[256,1024]{1,0:T(8,128)(2,1)S(1)} copy-done((bf16[256,1024]{1,0:T(8,128)(2,1)S(1)}, bf16[256,1024]{1,0:T(8,128)(2,1)}, u32[]{:S(2)}) %copy-start) | copy-done | bytes 524312
  1.7 0.0 copy-start.1
  1.7 0.9 %copy-done.1 = bf16[256,256]{1,0:T(8,128)(2,1)S(1)} copy-done((bf16[256,256]{1,0:T(8,128)(2,1)S(1)}, bf16[256,256]{1,0:T(8,128)(2,1)}, u32[]{:S(2)}) %copy-start.1) | copy-done | bytes 131096
  2.6 57.6 %shard_map.58 = (bf16[256,256]{1,0:T(8,128)(2,1)S(1)}, bf16[2048,1024]{1,0:T(8,128)(2,1)S(1)}, f32[1,256]{1,0:T(1,128)S(1)}) custom-call(bf16[256,256]{1,0:T(8,128)(2,1)S(1)} %copy-done.1, bf16[4096,1024]{1,0:T(8,128)(2,1)} %w_hbm.1, bf16[256,1024]{1,0:T(8,128)(2,1)S(1)} %copy-done), custom_call_target="tpu_custom_call" | custom-call | flops 6442450944 | bytes 12582912 | tf_op jit(solution)/shard_map/pallas_call | solution.py:319
  60.2 0.7 %copy.9 = bf16[256,256]{1,0:T(8,128)(2,1)} copy(bf16[256,256]{1,0:T(8,128)(2,1)S(1)} %get-tuple-element.12) | data formatting | bytes 262144
  60.8 2.0 %copy.10 = bf16[2048,1024]{1,0:T(8,128)(2,1)} copy(bf16[2048,1024]{1,0:T(8,128)(2,1)S(1)} %get-tuple-element.13) | data formatting | bytes 8388608
  62.8 0.6 copy.11
Async XLA Ops:
  0.6 1.0 %copy-start = (bf16[256,1024]{1,0:T(8,128)(2,1)S(1)}, bf16[256,1024]{1,0:T(8,128)(2,1)}, u32[]{:S(2)}) copy-start(bf16[256,1024]{1,0:T(8,128)(2,1)} %t.1) | copy-start | bytes 1572868
  1.7 0.9 %copy-start.1 = (bf16[256,256]{1,0:T(8,128)(2,1)S(1)}, bf16[256,256]{1,0:T(8,128)(2,1)}, u32[]{:S(2)}) copy-start(bf16[256,256]{1,0:T(8,128)(2,1)} %h_ref.1) | copy-start | bytes 393220

commit v4 on v3

--- a/solution.py
+++ b/solution.py
@@ -18,9 +18,9 @@
 
 def stages(h_ref, w_hbm, t, hg_ref, wg_ref, mm_ref,
            gath, pgath, w, es, et, score, cols, rowsbuf, stat,
-           sa, ra, sb, rb, pp, sd, rd,
+           sx, rx, sy, ry, sj, rj, pp, sd, rd,
            loc_sem, ag_recv, z_send, xy_send, f_send, st_send, st_recv,
-           a_send, a_recv, b_send, b_recv, d_send, d_recv, p_send, p_recv):
+           x_send, x_recv, y_send, y_recv, j_send, j_recv, d_send, d_recv, p_send, p_recv):
     n = gath.shape[0]
     tok, width = h_ref.shape
     half = tok // 2
@@ -65,13 +65,11 @@
                         device_id_type=pl.DeviceIdType.MESH)
     pl.semaphore_wait(barrier, n)
 
-    def piece(slot, h):
-        return gath.at[slot, pl.ds(h * half, half)]
-
     def gcopy(slot, h, ss, target):
-        return remote(piece(slot, h), piece(slot, h), ss, ag_recv.at[slot, h], target)
-
-    def wait_piece(slot, h):
+        ref = gath.at[slot] if h is None else gath.at[slot, pl.ds(h * half, half)]
+        return remote(ref, ref, ss, ag_recv.at[slot, h or 0], target)
+
+    def wait_piece(slot, h=None):
         gcopy(slot, h, f_send.at[0, 0], xdev).wait_recv()
 
     pending, pending_mid = [], []
@@ -86,16 +84,14 @@
 
     def fan_out(i):
         slot = dev(planes[i], 0, 0)
-        go(gcopy(slot, 0, xy_send.at[i, 0], ydev))
-        go(gcopy(slot, 1, xy_send.at[i, 1], xdev))
-        go(gcopy(slot, 1, xy_send.at[i, 2], ydev))
-        go(gcopy(slot, 0, xy_send.at[i, 3], xdev))
+        go(gcopy(slot, None, xy_send.at[i, 0], ydev))
+        go(gcopy(slot, None, xy_send.at[i, 1], xdev))
 
     def forward(i):
         s0, s1 = dev(planes[i], 1, 0), dev(planes[i], 0, 1)
-        wait_piece(s0, 0)
+        wait_piece(s0)
         go(gcopy(s0, 0, f_send.at[i, 0], xdev))
-        wait_piece(s1, 1)
+        wait_piece(s1)
         go(gcopy(s1, 1, f_send.at[i, 1], ydev))
 
     def wrows(slot, count):
@@ -110,9 +106,7 @@
             es[...] += part
 
     def plane(i):
-        s0, s1, s = dev(planes[i], 1, 0), dev(planes[i], 0, 1), dev(planes[i], 1, 1)
-        wait_piece(s0, 1)
-        wait_piece(s1, 0)
+        s = dev(planes[i], 1, 1)
         if i == 3:
             multiply(planes[3] * 4 + 2 * y, 2)
         wait_piece(s, 0)
@@ -123,9 +117,8 @@
             multiply(planes[i] * 4, 4, i == 0)
 
     zn_dev, zi_dev = dev(z_near, 0, 0), dev(z_in, 0, 0)
-    for h in range(2):
-        go(gcopy(me, h, z_send.at[0, h], zn_dev))
-        go_mid(gcopy(me, h, z_send.at[1, h], zi_dev))
+    go(gcopy(me, None, z_send.at[0], zn_dev))
+    go_mid(gcopy(me, None, z_send.at[1], zi_dev))
     fan_out(0)
 
     block = 32
@@ -146,9 +139,8 @@
     for i in range(1, 4):
         slot = dev(planes[i], 0, 0)
         target = zi_dev if i == 1 else zn_dev
-        for h in range(2):
-            wait_piece(slot, h)
-            go_mid(gcopy(slot, h, z_send.at[1 + i, h], target))
+        wait_piece(slot)
+        go_mid(gcopy(slot, None, z_send.at[1 + i], target))
         fan_out(i)
         forward(i - 1)
         if i > 1:
@@ -230,21 +222,25 @@
     near, beside, across, diag = block_of(0, 0), block_of(1, 0), block_of(0, 1), block_of(1, 1)
     top, bottom = pl.ds(0, half), pl.ds(half, half)
 
-    def bcopy(k, d, h):
-        return remote(sb.at[k, d, h], rb.at[k, d, h], b_send.at[k, d, h],
-                      b_recv.at[k, d, h], xdev if d else ydev)
+    def xcopy(k):
+        return remote(sx.at[k], rx.at[k], x_send.at[k], x_recv.at[k], xdev)
+
+    def ycopy(k):
+        return remote(sy.at[k], ry.at[k], y_send.at[k], y_recv.at[k], ydev)
+
+    def jcopy(k, d):
+        return remote(sj.at[k, d], rj.at[k, d], j_send.at[k, d], j_recv.at[k, d],
+                      xdev if d else ydev)
 
     for k in range(4):
         pp[k] = lax.dot_general(score[:tok, :], w[wrows(order[k] * 4, 4), :], NT,
                                 preferred_element_type=f32)
-        sa[k, 0] = pp[k, top, diag].astype(bf16)
-        sa[k, 1] = pp[k, bottom, diag].astype(bf16)
-        go(remote(sa.at[k, 0], ra.at[k, 0], a_send.at[k, 0], a_recv.at[k, 0], xdev))
-        go(remote(sa.at[k, 1], ra.at[k, 1], a_send.at[k, 1], a_recv.at[k, 1], ydev))
-        sb[k, 0, 1] = pp[k, bottom, beside].astype(bf16)
-        go(bcopy(k, 0, 1))
-        sb[k, 1, 0] = pp[k, top, across].astype(bf16)
-        go(bcopy(k, 1, 0))
+        sx[k, 0] = pp[k, top, diag].astype(bf16)
+        sx[k, 1] = pp[k, top, across].astype(bf16)
+        go(xcopy(k))
+        sy[k, 0] = pp[k, bottom, diag].astype(bf16)
+        sy[k, 1] = pp[k, bottom, beside].astype(bf16)
+        go(ycopy(k))
 
     pair = 2
 
@@ -260,34 +256,41 @@
         return c
 
     def join(k):
-        a = remote(sa.at[k, 0], ra.at[k, 0], a_send.at[k, 0], a_recv.at[k, 0], xdev)
-        a.wait_recv()
-        sb[k, 0, 0] = (pp[k, top, beside] + ra[k, 0].astype(f32)).astype(bf16)
-        go(bcopy(k, 0, 0))
-        a = remote(sa.at[k, 1], ra.at[k, 1], a_send.at[k, 1], a_recv.at[k, 1], ydev)
-        a.wait_recv()
-        sb[k, 1, 1] = (pp[k, bottom, across] + ra[k, 1].astype(f32)).astype(bf16)
-        go(bcopy(k, 1, 1))
-
-    join(0)
-    join(1)
-    ph.wait()
-    ps.wait()
-    lax.fori_loop(0, mine // (2 * pair), weight_part, 0)
-    join(2)
-    join(3)
-    lax.fori_loop(mine // (2 * pair), mine // pair, weight_part, 0)
-
-    for k in range(4):
-        for d in range(2):
-            for h in range(2):
-                bcopy(k, d, h).wait_recv()
-        for h in range(2):
-            hs = bottom if h else top
-            pp[k, hs, near] += rb[k, 0, h].astype(f32) + rb[k, 1, h].astype(f32)
+        xcopy(k).wait_recv()
+        sj[k, 0] = (pp[k, top, beside] + rx[k, 0].astype(f32)).astype(bf16)
+        go(jcopy(k, 0))
+        ycopy(k).wait_recv()
+        sj[k, 1] = (pp[k, bottom, across] + ry[k, 0].astype(f32)).astype(bf16)
+        go(jcopy(k, 1))
+
+    def column(k):
+        jcopy(k, 0).wait_recv()
+        pp[k, top, near] += rj[k, 0].astype(f32) + rx[k, 1].astype(f32)
+        jcopy(k, 1).wait_recv()
+        pp[k, bottom, near] += rj[k, 1].astype(f32) + ry[k, 1].astype(f32)
         if k < 3:
             sd[k] = pp[k, :, near].astype(bf16)
             go(remote(sd.at[k], rd.at[z], d_send.at[k], d_recv.at[z], dev(order[k], 0, 0)))
+
+    chunks = mine // pair
+
+    def wait_partner():
+        ph.wait()
+        ps.wait()
+
+    join(0)
+    join(1)
+    pl.when(core == 0)(wait_partner)
+    lax.fori_loop(0, (1 - core) * (chunks // 2), weight_part, 0)
+    join(2)
+    join(3)
+    column(0)
+    lax.fori_loop((1 - core) * (chunks // 2), (1 - core) * chunks, weight_part, 0)
+    column(1)
+    column(2)
+    pl.when(core == 1)(wait_partner)
+    lax.fori_loop(0, core * chunks, weight_part, 0)
+    column(3)
     total = pp[3, :, near]
     for k in range(3):
         zz = order[k]
@@ -337,22 +340,26 @@
             vm((n, 8, tok), f32),
             vm((4, 2, half, width), bf16),
             vm((4, 2, half, width), bf16),
-            vm((4, 2, 2, half, width), bf16),
-            vm((4, 2, 2, half, width), bf16),
+            vm((4, 2, half, width), bf16),
+            vm((4, 2, half, width), bf16),
+            vm((4, 2, half, width), bf16),
+            vm((4, 2, half, width), bf16),
             vm((4, tok, 4 * width), f32),
             vm((3, tok, width), bf16),
             vm((4, tok, width), bf16),
             dma((1,)),
             dma((n, 2)),
-            dma((5, 2)),
-            dma((4, 4)),
+            dma((5,)),
+            dma((4, 2)),
             dma((4, 2)),
             dma((n,)),
             dma((n,)),
+            dma((4,)),
+            dma((4,)),
+            dma((4,)),
+            dma((4,)),
             dma((4, 2)),
             dma((4, 2)),
-            dma((4, 2, 2)),
-            dma((4, 2, 2)),
             dma((3,)),
             dma((4,)),
             dma((2,)),

time: 63.6 us -> 63.4 us (level)
  no operation moved by 1% of the time
where the time goes in v4:
time: 63.4 us; the launch traced here: 63.2 us
  Pallas kernels  57.4 us (91%)
  local copies, waits for them, and re-layouts  5.17 us (8%)
  between operations  0.65 us (1%)
    pallas_call x1, Pallas kernels, fused(): pl.pallas_call(stages, out_shape=(jax.ShapeDtypeStruct((tok, width), bf16...  57.4 us
    unnamed x7, local copies, waits for them, and re-layouts  5.17 us

profile of v4, /device:TPU:0, one launch (start us, length us, event | category | flops | bytes accessed | tf_op | source)
XLA Modules:
  0.0 63.2 jit_solution(6841062674864047004)
XLA Ops:
  0.6 0.0 copy-start
  0.6 1.0 %copy-done = bf16[256,1024]{1,0:T(8,128)(2,1)S(1)} copy-done((bf16[256,1024]{1,0:T(8,128)(2,1)S(1)}, bf16[256,1024]{1,0:T(8,128)(2,1)}, u32[]{:S(2)}) %copy-start) | copy-done | bytes 524312
  1.7 0.0 copy-start.1
  1.7 0.9 %copy-done.1 = bf16[256,256]{1,0:T(8,128)(2,1)S(1)} copy-done((bf16[256,256]{1,0:T(8,128)(2,1)S(1)}, bf16[256,256]{1,0:T(8,128)(2,1)}, u32[]{:S(2)}) %copy-start.1) | copy-done | bytes 131096
  2.6 57.4 %shard_map.58 = (bf16[256,256]{1,0:T(8,128)(2,1)S(1)}, bf16[2048,1024]{1,0:T(8,128)(2,1)S(1)}, f32[1,256]{1,0:T(1,128)S(1)}) custom-call(bf16[256,256]{1,0:T(8,128)(2,1)S(1)} %copy-done.1, bf16[4096,1024]{1,0:T(8,128)(2,1)} %w_hbm.1, bf16[256,1024]{1,0:T(8,128)(2,1)S(1)} %copy-done), custom_call_target="tpu_custom_call" | custom-call | flops 6442450944 | bytes 12582912 | tf_op jit(solution)/shard_map/pallas_call | solution.py:322
  60.0 0.7 %copy.9 = bf16[256,256]{1,0:T(8,128)(2,1)} copy(bf16[256,256]{1,0:T(8,128)(2,1)S(1)} %get-tuple-element.12) | data formatting | bytes 262144
  60.7 2.0 %copy.10 = bf16[2048,1024]{1,0:T(8,128)(2,1)} copy(bf16[2048,1024]{1,0:T(8,128)(2,1)S(1)} %get-tuple-element.13) | data formatting | bytes 8388608
  62.7 0.6 copy.11
Async XLA Ops:
  0.6 1.0 %copy-start = (bf16[256,1024]{1,0:T(8,128)(2,1)S(1)}, bf16[256,1024]{1,0:T(8,128)(2,1)}, u32[]{:S(2)}) copy-start(bf16[256,1024]{1,0:T(8,128)(2,1)} %t.1) | copy-start | bytes 1572868
  1.7 0.9 %copy-start.1 = (bf16[256,256]{1,0:T(8,128)(2,1)S(1)}, bf16[256,256]{1,0:T(8,128)(2,1)}, u32[]{:S(2)}) copy-start(bf16[256,256]{1,0:T(8,128)(2,1)} %h_ref.1) | copy-start | bytes 393220

commit v5 on v2

--- a/solution.py
+++ b/solution.py
@@ -17,13 +17,13 @@
 BATCHES = 2
 
 
-def stages(h_hbm, w_hbm, t_hbm, hg_ref, wg_hbm, mm_ref,
-           gath, pgath, w, t, es, et, score, pscore, cols, rowsbuf, stat,
-           sa, ra, sb, rb, pb, q, sd, rd, wgs,
+def stages(h_ref, w_hbm, t, hg_ref, wg_ref, mm_ref,
+           gath, pgath, w, es, et, score, cols, rowsbuf, stat,
+           sx, rx, sy, ry, sj, rj, pp, sd, rd,
            loc_sem, ag_recv, z_send, xy_send, f_send, st_send, st_recv,
-           a_send, a_recv, b_send, b_recv, d_send, d_recv, p_send, p_recv, out_sem):
+           x_send, x_recv, y_send, y_recv, j_send, j_recv, d_send, d_recv, p_send, p_recv):
     n = gath.shape[0]
-    tok, width = h_hbm.shape
+    tok, width = h_ref.shape
     batch = tok // BATCHES
     half = batch // 2
     me = lax.axis_index("vocab")
@@ -54,12 +54,9 @@
             src_ref=src, dst_ref=dst, send_sem=p_send.at[i], recv_sem=p_recv.at[i],
             device_id={"rows": 1 - core}, device_id_type=pl.DeviceIdType.MESH)
 
-    cp_h = pltpu.make_async_copy(h_hbm, gath.at[me], loc_sem.at[0])
-    cp_w = pltpu.make_async_copy(w_hbm, w, loc_sem.at[1])
-    cp_t = pltpu.make_async_copy(t_hbm, t, loc_sem.at[2])
-    cp_h.start()
-    cp_t.start()
+    cp_w = pltpu.make_async_copy(w_hbm, w, loc_sem.at[0])
     cp_w.start()
+    gath[me] = h_ref[...]
 
     barrier = pltpu.get_barrier_semaphore()
 
@@ -71,7 +68,6 @@
     pl.semaphore_signal(barrier, inc=1, device_id={"rows": 1 - core},
                         device_id_type=pl.DeviceIdType.MESH)
     pl.semaphore_wait(barrier, n)
-    cp_h.wait()
 
     pending, pending_mid = [], []
 
@@ -84,62 +80,58 @@
         pending_mid.append(c)
 
     def gcopy(b, slot, h, ss, target):
-        ref = gath.at[slot, pl.ds(b * batch + h * half, half)]
-        return remote(ref, ref, ss, ag_recv.at[slot, b, h], target)
-
-    def wait_piece(b, slot, h):
+        start, size = (b * batch, batch) if h is None else (b * batch + h * half, half)
+        ref = gath.at[slot, pl.ds(start, size)]
+        return remote(ref, ref, ss, ag_recv.at[slot, b, h or 0], target)
+
+    def wait_piece(b, slot, h=None):
         gcopy(b, slot, h, f_send.at[b, 0, 0], xdev).wait_recv()
 
     def z_start(b):
-        for h in range(2):
-            go(gcopy(b, me, h, z_send.at[b, 0, h], zn_dev))
-            go_mid(gcopy(b, me, h, z_send.at[b, 1, h], zi_dev))
+        go(gcopy(b, me, None, z_send.at[b, 0], zn_dev))
+        go_mid(gcopy(b, me, None, z_send.at[b, 1], zi_dev))
 
     def z_step(b, i):
         slot = dev(planes[i], 0, 0)
-        for h in range(2):
-            wait_piece(b, slot, h)
-            go_mid(gcopy(b, slot, h, z_send.at[b, 1 + i, h], zi_dev if i == 1 else zn_dev))
+        wait_piece(b, slot)
+        go_mid(gcopy(b, slot, None, z_send.at[b, 1 + i], zi_dev if i == 1 else zn_dev))
 
     def fan_out(b, i):
         slot = dev(planes[i], 0, 0)
-        go(gcopy(b, slot, 0, xy_send.at[b, i, 0], ydev))
-        go(gcopy(b, slot, 1, xy_send.at[b, i, 1], xdev))
-        go(gcopy(b, slot, 1, xy_send.at[b, i, 2], ydev))
-        go(gcopy(b, slot, 0, xy_send.at[b, i, 3], xdev))
+        go(gcopy(b, slot, None, xy_send.at[b, i, 0], ydev))
+        go(gcopy(b, slot, None, xy_send.at[b, i, 1], xdev))
 
     def forward(b, i):
         s0, s1 = dev(planes[i], 1, 0), dev(planes[i], 0, 1)
-        wait_piece(b, s0, 0)
+        wait_piece(b, s0)
         go(gcopy(b, s0, 0, f_send.at[b, i, 0], xdev))
-        wait_piece(b, s1, 1)
+        wait_piece(b, s1)
         go(gcopy(b, s1, 1, f_send.at[b, i, 1], ydev))
 
-    def wrows(slot):
-        return pl.ds(pl.multiple_of(slot * width, width), width)
+    def wrows(slot, count):
+        return pl.ds(pl.multiple_of(slot * width, width), count * width)
 
     def brows(b):
         return pl.ds(b * batch, batch)
 
-    def multiply(b, slot, first=False):
-        part = jnp.dot(gath[slot, brows(b), :], w[wrows(slot), :], preferred_element_type=f32)
+    def multiply(b, slot, count, first=False):
+        a = jnp.concatenate([gath[slot + c, brows(b), :] for c in range(count)], axis=1)
+        part = jnp.dot(a, w[wrows(slot, count), :], preferred_element_type=f32)
         if first:
             es[brows(b), :] = part
         else:
             es[brows(b), :] += part
 
-    def sides(b, i):
-        s0, s1 = dev(planes[i], 1, 0), dev(planes[i], 0, 1)
-        wait_piece(b, s0, 1)
-        multiply(b, s0)
-        wait_piece(b, s1, 0)
-        multiply(b, s1)
-
-    def diagonal(b, i):
+    def plane(b, i):
         s = dev(planes[i], 1, 1)
+        if i == 3:
+            multiply(b, planes[3] * 4 + 2 * y, 2)
         wait_piece(b, s, 0)
         wait_piece(b, s, 1)
-        multiply(b, s)
+        if i == 3:
+            multiply(b, planes[3] * 4 + 2 * (1 - y), 2)
+        else:
+            multiply(b, planes[i] * 4, 4, i == 0)
 
     block = 32
     nblk = batch // block
@@ -212,61 +204,53 @@
         cols[brows(b), :] = jnp.transpose(rowsbuf[b])
         lax.fori_loop(b * nblk, (b + 1) * nblk, derive, 0)
 
-    def part(b, slot):
-        return lax.dot_general(score[brows(b), :], w[wrows(slot), :], NT,
-                               preferred_element_type=f32)
-
-    def acopy(b, k, h):
-        return remote(sa.at[b, k, h], ra.at[b, k, h], a_send.at[b, k, h],
-                      a_recv.at[b, k, h], ydev if h else xdev)
-
-    def bcopy(b, k, d, h):
-        return remote(sb.at[b, k, d, h], rb.at[b, k, d, h], b_send.at[b, k, d, h],
-                      b_recv.at[b, k, d, h], xdev if d else ydev)
+    def block_of(dy, dx):
+        return pl.ds(pl.multiple_of(dev(0, dy, dx) * width, width), width)
+
+    near, beside, across, diag = block_of(0, 0), block_of(1, 0), block_of(0, 1), block_of(1, 1)
+    top, bottom = pl.ds(0, half), pl.ds(half, half)
+
+    def xcopy(b, k):
+        return remote(sx.at[b, k], rx.at[b, k], x_send.at[b, k], x_recv.at[b, k], xdev)
+
+    def ycopy(b, k):
+        return remote(sy.at[b, k], ry.at[b, k], y_send.at[b, k], y_recv.at[b, k], ydev)
+
+    def jcopy(b, k, d):
+        return remote(sj.at[b, k, d], rj.at[b, k, d], j_send.at[b, k, d], j_recv.at[b, k, d],
+                      xdev if d else ydev)
 
     def spread(b):
         for k in range(4):
-            p = part(b, dev(order[k], 1, 1)).astype(bf16)
-            sa[b, k, 0] = p[:half]
-            sa[b, k, 1] = p[half:]
-            go(acopy(b, k, 0))
-            go(acopy(b, k, 1))
-        for k in range(4):
-            p = part(b, dev(order[k], 1, 0))
-            pb[b, k, 0] = p[:half]
-            sb[b, k, 0, 1] = p[half:].astype(bf16)
-            go(bcopy(b, k, 0, 1))
-            p = part(b, dev(order[k], 0, 1))
-            pb[b, k, 1] = p[half:]
-            sb[b, k, 1, 0] = p[:half].astype(bf16)
-            go(bcopy(b, k, 1, 0))
-
-    def home(b):
-        for k in range(4):
-            q[b, k] = part(b, dev(order[k], 0, 0))
+            pp[b, k] = lax.dot_general(score[brows(b), :], w[wrows(order[k] * 4, 4), :], NT,
+                                       preferred_element_type=f32)
+            sx[b, k, 0] = pp[b, k, top, diag].astype(bf16)
+            sx[b, k, 1] = pp[b, k, top, across].astype(bf16)
+            go(xcopy(b, k))
+            sy[b, k, 0] = pp[b, k, bottom, diag].astype(bf16)
+            sy[b, k, 1] = pp[b, k, bottom, beside].astype(bf16)
+            go(ycopy(b, k))
 
     def join(b, k):
-        acopy(b, k, 0).wait_recv()
-        sb[b, k, 0, 0] = (pb[b, k, 0] + ra[b, k, 0].astype(f32)).astype(bf16)
-        go(bcopy(b, k, 0, 0))
-        acopy(b, k, 1).wait_recv()
-        sb[b, k, 1, 1] = (pb[b, k, 1] + ra[b, k, 1].astype(f32)).astype(bf16)
-        go(bcopy(b, k, 1, 1))
+        xcopy(b, k).wait_recv()
+        sj[b, k, 0] = (pp[b, k, top, beside] + rx[b, k, 0].astype(f32)).astype(bf16)
+        go(jcopy(b, k, 0))
+        ycopy(b, k).wait_recv()
+        sj[b, k, 1] = (pp[b, k, bottom, across] + ry[b, k, 0].astype(f32)).astype(bf16)
+        go(jcopy(b, k, 1))
 
     def column(b, k):
-        for d in range(2):
-            for h in range(2):
-                bcopy(b, k, d, h).wait_recv()
-        for h in range(2):
-            hs = pl.ds(h * half, half)
-            q[b, k, hs, :] += rb[b, k, 0, h].astype(f32) + rb[b, k, 1, h].astype(f32)
+        jcopy(b, k, 0).wait_recv()
+        pp[b, k, top, near] += rj[b, k, 0].astype(f32) + rx[b, k, 1].astype(f32)
+        jcopy(b, k, 1).wait_recv()
+        pp[b, k, bottom, near] += rj[b, k, 1].astype(f32) + ry[b, k, 1].astype(f32)
         if k < 3:
-            sd[b, k] = q[b, k].astype(bf16)
+            sd[b, k] = pp[b, k, :, near].astype(bf16)
             go(remote(sd.at[b, k], rd.at[b, z], d_send.at[b, k], d_recv.at[b, z],
                       dev(order[k], 0, 0)))
 
     def finish(b):
-        total = q[b, 3]
+        total = pp[b, 3, :, near]
         for k in range(3):
             zz = order[k]
             remote(sd.at[b, k], rd.at[b, zz], d_send.at[b, k], d_recv.at[b, zz],
@@ -276,85 +260,79 @@
 
     mine = n // 2
 
-    def out_copy(j):
-        return pltpu.make_async_copy(
-            wgs.at[j], wg_hbm.at[pl.ds(pl.multiple_of(j * width, width), width)], out_sem.at[j])
+    pair = 2
+    chunks = mine // pair
 
     def weight_part(j, c):
-        slot = core * mine + j
+        slot = core * mine + j * pair
+        a = jnp.concatenate(
+            [jnp.concatenate([gath[slot + i], pgath[j * pair + i]], axis=0) for i in range(pair)],
+            axis=1)
         for v in range(2):
             vs = pl.ds(v * (w.shape[1] // 2), w.shape[1] // 2)
-            g = lax.dot_general(gath[slot], score[:, vs], TN, preferred_element_type=f32)
-            g += lax.dot_general(pgath[j], pscore[:, vs], TN, preferred_element_type=f32)
-            wgs[j, :, vs] = g.astype(bf16)
-        out_copy(j).start()
+            g = lax.dot_general(a, score[:, vs], TN, preferred_element_type=f32)
+            wg_ref[pl.ds(pl.multiple_of(j * pair * width, width), pair * width), vs] = g.astype(bf16)
         return c
 
     z_start(0)
     fan_out(0, 0)
     z_start(1)
     rowsbuf[...] = jnp.zeros_like(rowsbuf)
-    cp_t.wait()
     lax.fori_loop(0, BATCHES * nblk, teacher, 0)
-    cp_w.wait()
-    multiply(0, me, True)
     for i in range(1, 4):
         z_step(0, i)
         fan_out(0, i)
         z_step(1, i)
         forward(0, i - 1)
-        multiply(0, dev(planes[i], 0, 0))
         if i > 1:
-            sides(0, i - 2)
+            if i == 2:
+                cp_w.wait()
+            plane(0, i - 2)
     forward(0, 3)
     for i in range(4):
         fan_out(1, i)
-    diagonal(0, 0)
-    diagonal(0, 1)
+    plane(0, 2)
+    plane(0, 3)
+    stat_send(0)
     forward(1, 0)
-    sides(0, 2)
-    diagonal(0, 2)
-    sides(0, 3)
-    diagonal(0, 3)
-    stat_send(0)
     forward(1, 1)
-    multiply(1, me, True)
-    multiply(1, dev(planes[1], 0, 0))
-    sides(1, 0)
+    plane(1, 0)
     forward(1, 2)
+    forward(1, 3)
     stat_join(0)
-    forward(1, 3)
     spread(0)
-    multiply(1, dev(planes[2], 0, 0))
-    multiply(1, dev(planes[3], 0, 0))
-    for i in range(4):
-        if i:
-            sides(1, i)
-        diagonal(1, i)
+    for i in range(1, 4):
+        plane(1, i)
     ph = partner(gath.at[pl.ds((1 - core) * mine, mine)], pgath, 0)
     ph.start()
     stat_send(1)
     for k in range(4):
         join(0, k)
-    home(0)
     stat_join(1)
-    ps = partner(score, pscore, 1)
+    ps = partner(score.at[pl.ds(0, tok)], score.at[pl.ds(tok, tok)], 1)
     ps.start()
     spread(1)
     for k in range(4):
         column(0, k)
-    home(1)
+
+    def wait_partner():
+        ph.wait()
+        ps.wait()
+
     join(1, 0)
     join(1, 1)
-    ph.wait()
-    ps.wait()
-    lax.fori_loop(0, mine // 2, weight_part, 0)
+    pl.when(core == 0)(wait_partner)
+    lax.fori_loop(0, (1 - core) * (chunks // 2), weight_part, 0)
     join(1, 2)
     join(1, 3)
     finish(0)
-    lax.fori_loop(mine // 2, mine, weight_part, 0)
-    for k in range(4):
-        column(1, k)
+    column(1, 0)
+    lax.fori_loop((1 - core) * (chunks // 2), (1 - core) * chunks, weight_part, 0)
+    column(1, 1)
+    column(1, 2)
+    pl.when(core == 1)(wait_partner)
+    lax.fori_loop(0, core * chunks, weight_part, 0)
+    column(1, 3)
     finish(1)
 
     for c in pending:
@@ -370,21 +348,6 @@
             stat_copy(b, i).wait_send()
         return c
     lax.fori_loop(1, n, stat_done, 0)
-
-    def out_done(j, c):
-        out_copy(j).wait()
-        return c
-    lax.fori_loop(0, mine, out_done, 0)
-
-
-def publish(*refs):
-    k = len(refs) // 2
-    sems = refs[-1]
-    copies = [pltpu.make_async_copy(refs[i], refs[k + i], sems.at[i]) for i in range(k)]
-    for c in copies:
-        c.start()
-    for c in copies:
-        c.wait()
 
 
 def fused(n, hidden, head_weight, mentor_outputs):
@@ -397,54 +360,52 @@
     dma = pltpu.SemaphoreType.DMA
     anyspace = pl.BlockSpec(memory_space=pl.ANY)
     vspace = pl.BlockSpec(memory_space=pltpu.VMEM)
-    hbm = pl.BlockSpec(memory_space=pltpu.HBM)
     shapes = (
         jax.ShapeDtypeStruct((tok, width), bf16),
         jax.ShapeDtypeStruct((feats // 2, voc), bf16),
         jax.ShapeDtypeStruct((1, tok), f32),
     )
-    made = pl.pallas_call(
+    hg, wg, mm = pl.pallas_call(
         stages,
         out_shape=shapes,
-        in_specs=[hbm] * 3,
-        out_specs=(vspace, anyspace, vspace),
+        in_specs=[vspace, anyspace, vspace],
+        out_specs=(vspace,) * 3,
         scratch_shapes=[
             vm((n, tok, width), bf16),
             vm((mine, tok, width), bf16),
             vm((feats, voc), bf16),
-            vm((tok, voc), bf16),
             vm((tok, voc), f32),
             vm((tok, voc), f32),
-            vm((tok, voc), bf16),
-            vm((tok, voc), bf16),
+            vm((2 * tok, voc), bf16),
             vm((tok, 128), f32),
             vm((nb, 128, batch), f32),
             vm((nb, n, 8, batch), f32),
             vm((nb, 4, 2, half, width), bf16),
             vm((nb, 4, 2, half, width), bf16),
-            vm((nb, 4, 2, 2, half, width), bf16),
-            vm((nb, 4, 2, 2, half, width), bf16),
-            vm((nb, 4, 2, half, width), f32),
-            vm((nb, 4, batch, width), f32),
+            vm((nb, 4, 2, half, width), bf16),
+            vm((nb, 4, 2, half, width), bf16),
+            vm((nb, 4, 2, half, width), bf16),
+            vm((nb, 4, 2, half, width), bf16),
+            vm((nb, 4, batch, 4 * width), f32),
             vm((nb, 3, batch, width), bf16),
             vm((nb, 4, batch, width), bf16),
-            vm((mine, width, voc), bf16),
-            dma((3,)),
+            dma((1,)),
             dma((n, nb, 2)),
-            dma((nb, 5, 2)),
-            dma((nb, 4, 4)),
+            dma((nb, 5)),
+            dma((nb, 4, 2)),
             dma((nb, 4, 2)),
             dma((nb, n)),
             dma((nb, n)),
+            dma((nb, 4)),
+            dma((nb, 4)),
+            dma((nb, 4)),
+            dma((nb, 4)),
             dma((nb, 4, 2)),
             dma((nb, 4, 2)),
-            dma((nb, 4, 2, 2)),
-            dma((nb, 4, 2, 2)),
             dma((nb, 3)),
             dma((nb, 4)),
             dma((2,)),
             dma((2,)),
-            dma((mine,)),
         ],
         compiler_params=pltpu.CompilerParams(
             collective_id=0, has_side_effects=True, vmem_limit_bytes=48 * 1024 * 1024),
@@ -452,13 +413,6 @@
             flops=6 * tok * feats * voc, transcendentals=2 * tok * voc,
             bytes_accessed=2 * feats * voc + feats * voc),
     )(hidden, head_weight, mentor_outputs)
-    hg, wg, mm = pl.pallas_call(
-        publish,
-        out_shape=shapes,
-        in_specs=[anyspace] * 3,
-        out_specs=(hbm,) * 3,
-        scratch_shapes=[dma((3,))],
-    )(*made)
     return hg, wg, mm.reshape(tok)
 
 

time: 204 us -> 66.3 us (0.33)
  Pallas kernels: 198 us -> 60.3 us
    pallas_call x2 -> x1, Pallas kernels: 198 us -> 60.3 us  [fused(): pl.pallas_call(stages, out_shape=shapes, in_specs=[vspace, anyspace, vspa...]
    unnamed x10 -> x7, local copies, waits for them, and re-layouts: 5.09 us -> 5.17 us
where the time goes in v5:
time: 66.3 us; the launch traced here: 66.2 us
  Pallas kernels  60.3 us (91%)
  local copies, waits for them, and re-layouts  5.17 us (8%)
    pallas_call x1, Pallas kernels, fused(): pl.pallas_call(stages, out_shape=shapes, in_specs=[vspace, anyspace, vspa...  60.3 us
    unnamed x7, local copies, waits for them, and re-layouts  5.17 us

profile of v5, /device:TPU:0, one launch (start us, length us, event | category | flops | bytes accessed | tf_op | source)
XLA Modules:
  0.0 66.2 jit_solution(1421627119164985445)
XLA Ops:
  0.6 0.0 copy-start
  0.6 1.0 %copy-done = bf16[256,1024]{1,0:T(8,128)(2,1)S(1)} copy-done((bf16[256,1024]{1,0:T(8,128)(2,1)S(1)}, bf16[256,1024]{1,0:T(8,128)(2,1)}, u32[]{:S(2)}) %copy-start) | copy-done | bytes 524312
  1.7 0.0 copy-start.1
  1.7 0.9 %copy-done.1 = bf16[256,256]{1,0:T(8,128)(2,1)S(1)} copy-done((bf16[256,256]{1,0:T(8,128)(2,1)S(1)}, bf16[256,256]{1,0:T(8,128)(2,1)}, u32[]{:S(2)}) %copy-start.1) | copy-done | bytes 131096
  2.6 60.3 %shard_map.58 = (bf16[256,256]{1,0:T(8,128)(2,1)S(1)}, bf16[2048,1024]{1,0:T(8,128)(2,1)S(1)}, f32[1,256]{1,0:T(1,128)S(1)}) custom-call(bf16[256,256]{1,0:T(8,128)(2,1)S(1)} %copy-done.1, bf16[4096,1024]{1,0:T(8,128)(2,1)} %w_hbm.1, bf16[256,1024]{1,0:T(8,128)(2,1)S(1)} %copy-done), custom_call_target="tpu_custom_call" | custom-call | flops 6442450944 | bytes 12582912 | tf_op jit(solution)/shard_map/pallas_call | solution.py:368
  62.9 0.7 copy.9
  63.6 2.0 %copy.10 = bf16[2048,1024]{1,0:T(8,128)(2,1)} copy(bf16[2048,1024]{1,0:T(8,128)(2,1)S(1)} %get-tuple-element.13) | data formatting | bytes 8388608
  65.6 0.6 copy.11
Async XLA Ops:
  0.6 1.0 %copy-start = (bf16[256,1024]{1,0:T(8,128)(2,1)S(1)}, bf16[256,1024]{1,0:T(8,128)(2,1)}, u32[]{:S(2)}) copy-start(bf16[256,1024]{1,0:T(8,128)(2,1)} %t.1) | copy-start | bytes 1572868
  1.7 0.9 %copy-start.1 = (bf16[256,256]{1,0:T(8,128)(2,1)S(1)}, bf16[256,256]{1,0:T(8,128)(2,1)}, u32[]{:S(2)}) copy-start(bf16[256,256]{1,0:T(8,128)(2,1)} %h_ref.1) | copy-start | bytes 393220

commit v6 on v4

--- a/solution.py
+++ b/solution.py
@@ -18,9 +18,9 @@
 
 def stages(h_ref, w_hbm, t, hg_ref, wg_ref, mm_ref,
            gath, pgath, w, es, et, score, cols, rowsbuf, stat,
-           sx, rx, sy, ry, sj, rj, pp, sd, rd,
+           sx, rx, sy, ry, sj, rj, sn, rn, pp, sd, rd,
            loc_sem, ag_recv, z_send, xy_send, f_send, st_send, st_recv,
-           x_send, x_recv, y_send, y_recv, j_send, j_recv, d_send, d_recv, p_send, p_recv):
+           x_send, x_recv, y_send, y_recv, j_send, j_recv, n_send, n_recv, d_send, d_recv, p_send, p_recv):
     n = gath.shape[0]
     tok, width = h_ref.shape
     half = tok // 2
@@ -91,8 +91,12 @@
         s0, s1 = dev(planes[i], 1, 0), dev(planes[i], 0, 1)
         wait_piece(s0)
         go(gcopy(s0, 0, f_send.at[i, 0], xdev))
+        if i == 0:
+            go(gcopy(s0, None, xy_send.at[1, 0], zn_dev))
         wait_piece(s1)
         go(gcopy(s1, 1, f_send.at[i, 1], ydev))
+        if i == 0:
+            go(gcopy(s1, None, xy_send.at[1, 1], zn_dev))
 
     def wrows(slot, count):
         return pl.ds(pl.multiple_of(slot * width, width), count * width)
@@ -141,7 +145,8 @@
         target = zi_dev if i == 1 else zn_dev
         wait_piece(slot)
         go_mid(gcopy(slot, None, z_send.at[1 + i], target))
-        fan_out(i)
+        if i > 1:
+            fan_out(i)
         forward(i - 1)
         if i > 1:
             if i == 2:
@@ -232,15 +237,46 @@
         return remote(sj.at[k, d], rj.at[k, d], j_send.at[k, d], j_recv.at[k, d],
                       xdev if d else ydev)
 
-    for k in range(4):
+    def xdiag(k):
+        return remote(sx.at[k, 0], rx.at[k, 0], x_send.at[k], x_recv.at[k], xdev)
+
+    def ydiag(k):
+        return remote(sy.at[k, 0], ry.at[k, 0], y_send.at[k], y_recv.at[k], ydev)
+
+    def ncopy(d):
+        return remote(sn.at[0, d], rn.at[0, d], n_send.at[0, d], n_recv.at[0, d], zn_dev)
+
+    def fcopy(d):
+        return remote(sn.at[1, d], rn.at[1, d], n_send.at[1, d], n_recv.at[1, d],
+                      xdev if d else ydev)
+
+    def home(k):
+        sd[k] = pp[k, :, near].astype(bf16)
+        go(remote(sd.at[k], rd.at[z], d_send.at[k], d_recv.at[z], dev(order[k], 0, 0)))
+
+    for k in (2, 3, 0, 1):
         pp[k] = lax.dot_general(score[:tok, :], w[wrows(order[k] * 4, 4), :], NT,
                                 preferred_element_type=f32)
         sx[k, 0] = pp[k, top, diag].astype(bf16)
-        sx[k, 1] = pp[k, top, across].astype(bf16)
-        go(xcopy(k))
         sy[k, 0] = pp[k, bottom, diag].astype(bf16)
-        sy[k, 1] = pp[k, bottom, beside].astype(bf16)
-        go(ycopy(k))
+        if k < 2:
+            sx[k, 1] = pp[k, top, across].astype(bf16)
+            sy[k, 1] = pp[k, bottom, beside].astype(bf16)
+            go(xcopy(k))
+            go(ycopy(k))
+        else:
+            go(xdiag(k))
+            go(ydiag(k))
+
+    def whole(k, i, copy):
+        xdiag(k).wait_recv()
+        sn[i, 0, top, :] = (pp[k, top, beside] + rx[k, 0].astype(f32)).astype(bf16)
+        sn[i, 0, bottom, :] = pp[k, bottom, beside].astype(bf16)
+        go(copy(0))
+        ydiag(k).wait_recv()
+        sn[i, 1, top, :] = pp[k, top, across].astype(bf16)
+        sn[i, 1, bottom, :] = (pp[k, bottom, across] + ry[k, 0].astype(f32)).astype(bf16)
+        go(copy(1))
 
     pair = 2
 
@@ -268,9 +304,7 @@
         pp[k, top, near] += rj[k, 0].astype(f32) + rx[k, 1].astype(f32)
         jcopy(k, 1).wait_recv()
         pp[k, bottom, near] += rj[k, 1].astype(f32) + ry[k, 1].astype(f32)
-        if k < 3:
-            sd[k] = pp[k, :, near].astype(bf16)
-            go(remote(sd.at[k], rd.at[z], d_send.at[k], d_recv.at[z], dev(order[k], 0, 0)))
+        home(k)
 
     chunks = mine // pair
 
@@ -278,19 +312,25 @@
         ph.wait()
         ps.wait()
 
+    whole(2, 0, ncopy)
     join(0)
     join(1)
+    home(2)
     pl.when(core == 0)(wait_partner)
     lax.fori_loop(0, (1 - core) * (chunks // 2), weight_part, 0)
-    join(2)
-    join(3)
+    ncopy(0).wait_recv()
+    pp[3, :, beside] += rn[0, 0].astype(f32)
+    ncopy(1).wait_recv()
+    pp[3, :, across] += rn[0, 1].astype(f32)
+    whole(3, 1, fcopy)
     column(0)
+    column(1)
     lax.fori_loop((1 - core) * (chunks // 2), (1 - core) * chunks, weight_part, 0)
-    column(1)
-    column(2)
     pl.when(core == 1)(wait_partner)
     lax.fori_loop(0, core * chunks, weight_part, 0)
-    column(3)
+    fcopy(0).wait_recv()
+    fcopy(1).wait_recv()
+    pp[3, :, near] += rn[1, 0].astype(f32) + rn[1, 1].astype(f32)
     total = pp[3, :, near]
     for k in range(3):
         zz = order[k]
@@ -344,6 +384,8 @@
             vm((4, 2, half, width), bf16),
             vm((4, 2, half, width), bf16),
             vm((4, 2, half, width), bf16),
+            vm((2, 2, tok, width), bf16),
+            vm((2, 2, tok, width), bf16),
             vm((4, tok, 4 * width), f32),
             vm((3, tok, width), bf16),
             vm((4, tok, width), bf16),
@@ -360,6 +402,8 @@
             dma((4,)),
             dma((4, 2)),
             dma((4, 2)),
+            dma((2, 2)),
+            dma((2, 2)),
             dma((3,)),
             dma((4,)),
             dma((2,)),

time: 63.4 us -> 67.3 us (1.062)
  Pallas kernels: 57.4 us -> 61.3 us
    pallas_call x1, Pallas kernels: 57.4 us -> 61.3 us  [fused(): pl.pallas_call(stages, out_shape=(jax.ShapeDtypeStruct((tok, width), bf16...]
where the time goes in v6:
time: 67.3 us; the launch traced here: 67.1 us
  Pallas kernels  61.3 us (91%)
  local copies, waits for them, and re-layouts  5.17 us (8%)
    pallas_call x1, Pallas kernels, fused(): pl.pallas_call(stages, out_shape=(jax.ShapeDtypeStruct((tok, width), bf16...  61.3 us
    unnamed x7, local copies, waits for them, and re-layouts  5.17 us

profile of v6, /device:TPU:0, one launch (start us, length us, event | category | flops | bytes accessed | tf_op | source)
XLA Modules:
  0.0 67.1 jit_solution(18238203736564328061)
XLA Ops:
  0.6 0.0 copy-start
  0.6 1.0 %copy-done = bf16[256,1024]{1,0:T(8,128)(2,1)S(1)} copy-done((bf16[256,1024]{1,0:T(8,128)(2,1)S(1)}, bf16[256,1024]{1,0:T(8,128)(2,1)}, u32[]{:S(2)}) %copy-start) | copy-done | bytes 524312
  1.7 0.0 copy-start.1
  1.7 0.9 %copy-done.1 = bf16[256,256]{1,0:T(8,128)(2,1)S(1)} copy-done((bf16[256,256]{1,0:T(8,128)(2,1)S(1)}, bf16[256,256]{1,0:T(8,128)(2,1)}, u32[]{:S(2)}) %copy-start.1) | copy-done | bytes 131096
  2.6 61.3 %shard_map.58 = (bf16[256,256]{1,0:T(8,128)(2,1)S(1)}, bf16[2048,1024]{1,0:T(8,128)(2,1)S(1)}, f32[1,256]{1,0:T(1,128)S(1)}) custom-call(bf16[256,256]{1,0:T(8,128)(2,1)S(1)} %copy-done.1, bf16[4096,1024]{1,0:T(8,128)(2,1)} %w_hbm.1, bf16[256,1024]{1,0:T(8,128)(2,1)S(1)} %copy-done), custom_call_target="tpu_custom_call" | custom-call | flops 6442450944 | bytes 12582912 | tf_op jit(solution)/shard_map/pallas_call | solution.py:362
  63.8 0.7 copy.9
  64.5 2.0 %copy.10 = bf16[2048,1024]{1,0:T(8,128)(2,1)} copy(bf16[2048,1024]{1,0:T(8,128)(2,1)S(1)} %get-tuple-element.13) | data formatting | bytes 8388608
  66.5 0.6 copy.11
Async XLA Ops:
  0.6 1.0 %copy-start = (bf16[256,1024]{1,0:T(8,128)(2,1)S(1)}, bf16[256,1024]{1,0:T(8,128)(2,1)}, u32[]{:S(2)}) copy-start(bf16[256,1024]{1,0:T(8,128)(2,1)} %t.1) | copy-start | bytes 1572868
  1.7 0.9 %copy-start.1 = (bf16[256,256]{1,0:T(8,128)(2,1)S(1)}, bf16[256,256]{1,0:T(8,128)(2,1)}, u32[]{:S(2)}) copy-start(bf16[256,256]{1,0:T(8,128)(2,1)} %h_ref.1) | copy-start | bytes 393220

commit v7 on v4

--- a/solution.py
+++ b/solution.py
@@ -18,9 +18,9 @@
 
 def stages(h_ref, w_hbm, t, hg_ref, wg_ref, mm_ref,
            gath, pgath, w, es, et, score, cols, rowsbuf, stat,
-           sx, rx, sy, ry, sj, rj, pp, sd, rd,
+           sx, rx, sy, ry, sj, rj, pp, sd, rd, zb,
            loc_sem, ag_recv, z_send, xy_send, f_send, st_send, st_recv,
-           x_send, x_recv, y_send, y_recv, j_send, j_recv, d_send, d_recv, p_send, p_recv):
+           x_send, x_recv, y_send, y_recv, j_send, j_recv, d_send, d_recv, e_send, e_recv, p_send, p_recv):
     n = gath.shape[0]
     tok, width = h_ref.shape
     half = tok // 2
@@ -263,14 +263,29 @@
         sj[k, 1] = (pp[k, bottom, across] + ry[k, 0].astype(f32)).astype(bf16)
         go(jcopy(k, 1))
 
+    def dcopy(k):
+        return remote(sd.at[k], rd.at[z], d_send.at[k], d_recv.at[z], dev(order[k], 0, 0))
+
+    def ecopy(k):
+        return remote(sd.at[k], zb.at[k], e_send.at[k], e_recv.at[k], zn_dev)
+
     def column(k):
         jcopy(k, 0).wait_recv()
         pp[k, top, near] += rj[k, 0].astype(f32) + rx[k, 1].astype(f32)
         jcopy(k, 1).wait_recv()
         pp[k, bottom, near] += rj[k, 1].astype(f32) + ry[k, 1].astype(f32)
+        if k < 2:
+            @pl.when(mid)
+            def _():
+                ecopy(k).wait_recv()
+                pp[k, :, near] += zb[k].astype(f32)
         if k < 3:
             sd[k] = pp[k, :, near].astype(bf16)
-            go(remote(sd.at[k], rd.at[z], d_send.at[k], d_recv.at[z], dev(order[k], 0, 0)))
+        if k < 2:
+            pl.when(mid)(dcopy(k).start)
+            pl.when(jnp.logical_not(mid))(ecopy(k).start)
+        elif k == 2:
+            go(dcopy(k))
 
     chunks = mine // pair
 
@@ -292,7 +307,7 @@
     lax.fori_loop(0, core * chunks, weight_part, 0)
     column(3)
     total = pp[3, :, near]
-    for k in range(3):
+    for k in range(1, 3):
         zz = order[k]
         remote(sd.at[k], rd.at[zz], d_send.at[k], d_recv.at[zz], dev(zz, 0, 0)).wait_recv()
         total += rd[zz].astype(f32)
@@ -305,6 +320,13 @@
     def _():
         for c in pending_mid:
             c.wait_send()
+        for k in range(2):
+            dcopy(k).wait_send()
+
+    @pl.when(jnp.logical_not(mid))
+    def _():
+        for k in range(2):
+            ecopy(k).wait_send()
 
     def stat_done(i, c):
         stat_copy(i).wait_send()
@@ -347,6 +369,7 @@
             vm((4, tok, 4 * width), f32),
             vm((3, tok, width), bf16),
             vm((4, tok, width), bf16),
+            vm((2, tok, width), bf16),
             dma((1,)),
             dma((n, 2)),
             dma((5,)),
@@ -362,6 +385,8 @@
             dma((4, 2)),
             dma((3,)),
             dma((4,)),
+            dma((2,)),
+            dma((2,)),
             dma((2,)),
             dma((2,)),
         ],

time: 63.4 us -> 66.6 us (1.050)
  Pallas kernels: 57.4 us -> 60.6 us
    pallas_call x1, Pallas kernels: 57.4 us -> 60.6 us  [fused(): pl.pallas_call(stages, out_shape=(jax.ShapeDtypeStruct((tok, width), bf16...]
where the time goes in v7:
time: 66.6 us; the launch traced here: 66.5 us
  Pallas kernels  60.6 us (91%)
  local copies, waits for them, and re-layouts  5.17 us (8%)
    pallas_call x1, Pallas kernels, fused(): pl.pallas_call(stages, out_shape=(jax.ShapeDtypeStruct((tok, width), bf16...  60.6 us
    unnamed x7, local copies, waits for them, and re-layouts  5.17 us

profile of v7, /device:TPU:0, one launch (start us, length us, event | category | flops | bytes accessed | tf_op | source)
XLA Modules:
  0.0 66.5 jit_solution(16821008363217153094)
XLA Ops:
  0.6 0.0 copy-start
  0.6 1.0 %copy-done = bf16[256,1024]{1,0:T(8,128)(2,1)S(1)} copy-done((bf16[256,1024]{1,0:T(8,128)(2,1)S(1)}, bf16[256,1024]{1,0:T(8,128)(2,1)}, u32[]{:S(2)}) %copy-start) | copy-done | bytes 524312
  1.7 0.0 copy-start.1
  1.7 0.9 %copy-done.1 = bf16[256,256]{1,0:T(8,128)(2,1)S(1)} copy-done((bf16[256,256]{1,0:T(8,128)(2,1)S(1)}, bf16[256,256]{1,0:T(8,128)(2,1)}, u32[]{:S(2)}) %copy-start.1) | copy-done | bytes 131096
  2.6 60.6 %shard_map.58 = (bf16[256,256]{1,0:T(8,128)(2,1)S(1)}, bf16[2048,1024]{1,0:T(8,128)(2,1)S(1)}, f32[1,256]{1,0:T(1,128)S(1)}) custom-call(bf16[256,256]{1,0:T(8,128)(2,1)S(1)} %copy-done.1, bf16[4096,1024]{1,0:T(8,128)(2,1)} %w_hbm.1, bf16[256,1024]{1,0:T(8,128)(2,1)S(1)} %copy-done), custom_call_target="tpu_custom_call" | custom-call | flops 6442450944 | bytes 12582912 | tf_op jit(solution)/shard_map/pallas_call | solution.py:344
  63.2 0.7 copy.9
  63.9 2.0 %copy.10 = bf16[2048,1024]{1,0:T(8,128)(2,1)} copy(bf16[2048,1024]{1,0:T(8,128)(2,1)S(1)} %get-tuple-element.13) | data formatting | bytes 8388608
  65.9 0.6 copy.11
Async XLA Ops:
  0.6 1.0 %copy-start = (bf16[256,1024]{1,0:T(8,128)(2,1)S(1)}, bf16[256,1024]{1,0:T(8,128)(2,1)}, u32[]{:S(2)}) copy-start(bf16[256,1024]{1,0:T(8,128)(2,1)} %t.1) | copy-start | bytes 1572868
  1.7 0.9 %copy-start.1 = (bf16[256,256]{1,0:T(8,128)(2,1)S(1)}, bf16[256,256]{1,0:T(8,128)(2,1)}, u32[]{:S(2)}) copy-start(bf16[256,256]{1,0:T(8,128)(2,1)} %h_ref.1) | copy-start | bytes 393220
